TPU v7x, 32 devices: a whole 2x2x4 slice. The times are simulated.
32 devices in a mesh: grp: 2 (over x), seq: 16 (over z, y, core).
Axes of the slice: x: 2, y: 2, z: 4, core: 2. Of those that a mesh axis runs over, the one named last changes fastest.
Arguments:
- activations: bfloat16 [16384, 1536], P(('grp', 'seq')), parts along dimension 0, may hold values from -60 to 60, as said below
- dilated_tap_weight: bfloat16 [3, 1536, 768], replicated, may hold values from -0.09375 to 0.09375
- conv_mix: bfloat16 [768, 1536], replicated, may hold values from -0.21875 to 0.21875
- w_query: bfloat16 [1536, 128], replicated, may hold values from -0.15625 to 0.15625
- w_keyval: bfloat16 [1536, 256], replicated, may hold values from -0.15625 to 0.15625
- contact_tiles: bfloat16 [16, 128, 128], replicated, may hold values from -8 to 250, as said below
- tile_codes: int32 [128, 65], P(('grp', 'seq')), parts along dimension 0, may hold values from 0 to 15
- bin_valid: int32 [16384], P('grp'), parts along dimension 0, may hold values 0 or 1
Outputs:
- attended: bfloat16 [16384, 128], P(('grp', 'seq')), parts along dimension 0
There are 2 independent parts, one for each index of `grp`. A program takes and returns all parts, laid end to end along the dimension named above; an argument that names none is the same for every part. Nothing has to cross between parts.
Inputs may be any that keep to these rules, and one draw needn't show every extreme that they name: `activations`: finite values. `contact_tiles`: finite values.
All inputs are finite; a program needn't handle non-finite values.
Results may differ from a plain program's by a relative error of at most 0.005.
Values may be sent and summed in bfloat16 or wider, within the bound.
A program may use at most 64 MiB of HBM per device.

v0:
```python
import math

import jax
import jax.numpy as jnp
from jax import lax
from jax.sharding import PartitionSpec as P

HDIM = 128
CONV_DILATION = 8
HALF = 4096


masked_score = -1e30
norm_eps = 1e-06


def padded(x, sides, width):
    for axis, dim in sides:
        size, length = (lax.axis_size(axis), x.shape[dim])
        up = [(i, (i + 1) % size) for i in range(size - 1)]
        down = [(j, i) for i, j in up]
        last = lax.slice_in_dim(x, length - width, length, axis=dim)
        initial = lax.slice_in_dim(x, 0, width, axis=dim)
        before = lax.ppermute(last, axis, up)
        after = lax.ppermute(initial, axis, down)
        x = jnp.concatenate([before, x, after], axis=dim)
    return x


def tile_bias(codes_local, contact_tiles, query_first, key_first, key_count):
    tile_size = contact_tiles.shape[1]
    code_count = contact_tiles.shape[0]
    offset_count = codes_local.shape[1]
    query_tiles_n = codes_local.shape[0]
    key_tiles_n = key_count // tile_size
    query_tiles = query_first + jnp.arange(query_tiles_n, dtype=jnp.int32)
    key_tiles = key_first + jnp.arange(key_tiles_n, dtype=jnp.int32)
    offset = jnp.clip(
        key_tiles[None, :] - query_tiles[:, None] + offset_count // 2, 0, offset_count - 1
    )
    slots = jnp.arange(offset_count, dtype=jnp.int32)
    picked = jnp.sum(
        jnp.where(offset[:, :, None] == slots[None, None, :], codes_local[:, None, :], 0), axis=2
    )
    picked_full = jnp.broadcast_to(
        picked[:, None, :, None], (query_tiles_n, tile_size, key_tiles_n, tile_size)
    ).reshape(query_tiles_n * tile_size, key_count)
    bias_block = jnp.zeros((query_tiles_n * tile_size, key_count), jnp.float32)
    for code in range(code_count):
        spread_tile = jnp.broadcast_to(
            contact_tiles[code][None, :, None, :],
            (query_tiles_n, tile_size, key_tiles_n, tile_size),
        ).reshape(query_tiles_n * tile_size, key_count)
        bias_block = jnp.where(picked_full == code, spread_tile.astype(jnp.float32), bias_block)
    return bias_block


def block_scores(
    query_heads, keyval, bin_valid, codes_local, contact_tiles, query_start, key_start, total_bins
):
    key_count = keyval.shape[0]
    query_rows, head_count, head_dim = query_heads.shape
    width_heads = head_count * head_dim
    tile_size = contact_tiles.shape[1]
    key_heads = keyval[:, :width_heads].reshape(key_count, head_count, head_dim)
    value_heads = keyval[:, width_heads:].reshape(key_count, head_count, head_dim)
    raw_scores = jnp.einsum(
        "qhd,khd->qhk", query_heads, key_heads, preferred_element_type=jnp.float32
    ) * (1.0 / math.sqrt(head_dim))
    bias_block = tile_bias(
        codes_local,
        contact_tiles,
        query_start // tile_size,
        jnp.floor_divide(key_start, tile_size),
        key_count,
    )
    key_pos = key_start + jnp.arange(key_count, dtype=jnp.int32)
    query_pos = query_start + jnp.arange(query_rows, dtype=jnp.int32)
    inside = (key_pos >= 0) & (key_pos < total_bins)
    valid_keys = lax.dynamic_slice_in_dim(
        bin_valid, jnp.clip(key_start, 0, total_bins - key_count), key_count
    )
    in_band = jnp.abs(key_pos[None, :] - query_pos[:, None]) <= HALF
    kept_pairs = (
        inside[None, :]
        & in_band
        & ((valid_keys[None, :] == 1) | (key_pos[None, :] == query_pos[:, None]))
    )
    scores = jnp.where(kept_pairs[:, None, :], raw_scores + bias_block[:, None, :], masked_score)
    return (scores, value_heads)


def absorb(softmax_state, pairs):
    row_peak, row_total, weighted = softmax_state
    new_peak = row_peak
    for scores, value_heads in pairs:
        new_peak = jnp.maximum(new_peak, jnp.max(scores, axis=-1))
    rescale = jnp.exp(row_peak - new_peak)
    row_total = row_total * rescale
    weighted = weighted * rescale[..., None]
    for scores, value_heads in pairs:
        probs = jnp.exp(scores - new_peak[..., None])
        row_total = row_total + jnp.sum(probs, axis=-1)
        weighted = weighted + jnp.einsum(
            "qhk,khd->qhd",
            probs.astype(jnp.bfloat16),
            value_heads,
            preferred_element_type=jnp.float32,
        )
    return (new_peak, row_total, weighted)


def per_device(
    activations,
    dilated_tap_weight,
    conv_mix,
    w_query,
    w_keyval,
    contact_tiles,
    tile_codes,
    bin_valid,
):
    genomic_bin_rows = activations.shape[0]
    seq_size = lax.axis_size("seq")
    position = lax.axis_index("seq")
    total_bins = seq_size * genomic_bin_rows
    query_start = position * genomic_bin_rows
    border_padded = padded(activations, (("seq", 0),), CONV_DILATION)
    raised_features = jax.nn.gelu(border_padded.astype(jnp.float32), approximate=False).astype(
        jnp.bfloat16
    )
    tap_low = jnp.dot(raised_features, dilated_tap_weight[0], preferred_element_type=jnp.float32)
    tap_mid = jnp.dot(raised_features, dilated_tap_weight[1], preferred_element_type=jnp.float32)
    tap_high = jnp.dot(raised_features, dilated_tap_weight[2], preferred_element_type=jnp.float32)
    conv_sum = (
        tap_low[0:genomic_bin_rows] + tap_mid[CONV_DILATION : CONV_DILATION + genomic_bin_rows]
    )
    conv_sum = conv_sum + tap_high[2 * CONV_DILATION : 2 * CONV_DILATION + genomic_bin_rows]
    squeezed = jax.nn.gelu(conv_sum, approximate=False).astype(jnp.bfloat16)
    mixed_rows = activations.astype(jnp.float32) + jnp.dot(
        squeezed, conv_mix, preferred_element_type=jnp.float32
    )
    normed = (
        mixed_rows * lax.rsqrt(jnp.mean(mixed_rows * mixed_rows, axis=-1, keepdims=True) + norm_eps)
    ).astype(jnp.bfloat16)
    queries = jnp.dot(normed, w_query, preferred_element_type=jnp.float32).astype(jnp.bfloat16)
    keyval = jnp.dot(normed, w_keyval, preferred_element_type=jnp.float32).astype(jnp.bfloat16)
    width_heads = queries.shape[1]
    head_count = w_keyval.shape[1] // (2 * HDIM)
    query_heads = queries.reshape(genomic_bin_rows, head_count, HDIM)
    reach = HALF // genomic_bin_rows

    def absorb_pair(softmax_state, from_below, from_above, distance):
        low_pair = block_scores(
            query_heads,
            from_below,
            bin_valid,
            tile_codes,
            contact_tiles,
            query_start,
            query_start - distance * genomic_bin_rows,
            total_bins,
        )
        high_pair = block_scores(
            query_heads,
            from_above,
            bin_valid,
            tile_codes,
            contact_tiles,
            query_start,
            query_start + distance * genomic_bin_rows,
            total_bins,
        )
        return absorb(softmax_state, (low_pair, high_pair))

    initial = (
        jnp.full((genomic_bin_rows, head_count), masked_score, jnp.float32),
        jnp.zeros((genomic_bin_rows, head_count), jnp.float32),
        jnp.zeros((genomic_bin_rows, head_count, HDIM), jnp.float32),
    )
    own_pair = block_scores(
        query_heads,
        keyval,
        bin_valid,
        tile_codes,
        contact_tiles,
        query_start,
        query_start,
        total_bins,
    )
    softmax_state = absorb(initial, (own_pair,))
    everything = lax.all_gather(keyval, "seq", axis=0, tiled=True)

    def collect_turn(distance, state_now):
        low_start = jnp.clip(
            query_start - distance * genomic_bin_rows, 0, total_bins - genomic_bin_rows
        )
        high_start = jnp.clip(
            query_start + distance * genomic_bin_rows, 0, total_bins - genomic_bin_rows
        )
        from_below = lax.dynamic_slice_in_dim(everything, low_start, genomic_bin_rows, 0)
        from_above = lax.dynamic_slice_in_dim(everything, high_start, genomic_bin_rows, 0)
        return absorb_pair(state_now, from_below, from_above, distance)

    softmax_state = lax.fori_loop(1, reach + 1, collect_turn, softmax_state)
    row_peak, row_total, weighted = softmax_state
    attended = (weighted / row_total[..., None]).reshape(genomic_bin_rows, width_heads)
    return attended.astype(jnp.bfloat16)


def solution(mesh):
    in_specs = (P(("grp", "seq"), None), P(), P(), P(), P(), P(), P(("grp", "seq"), None), P("grp"))
    out_specs = P(("grp", "seq"), None)
    return jax.shard_map(
        per_device, mesh=mesh, in_specs=in_specs, out_specs=out_specs, check_vma=False
    )
```

profile of v0, /device:TPU:18, one launch (start us, length us, event | category | flops | bytes accessed | tf_op | source)
XLA Modules:
  0.0 542.8 jit_solution(11341009575677297269)
XLA Ops:
  9.4 4.5 collective-permute-start.1
  15.4 8.1 %fusion.31 = bf16[528,1536]{1,0:T(8,128)(2,1)S(1)} fusion(bf16[8,1536]{1,0:T(8,128)(2,1)S(1)} %collective-permute-done.1, bf16[512,1536]{1,0:T(8,128)(2,1)} %param.10, bf16[8,1536]{1,0:T(8,128)(2,1)S(1)} %collective-permute-done), kind=kLoop, calls=%fused_computation.109 | loop fusion | flops 57581568 | bytes 3244032 | tf_op jit(solution)/shard_map/convert_element_type | solution.py:129
  23.6 4.8 fusion.61
  28.4 4.3 fusion.63
  32.6 11.6 %multiply_reduce_fusion = (f32[512]{0:T(512)S(1)}, f32[512,1536]{1,0:T(8,128)}) fusion(bf16[768,1536]{1,0:T(8,128)(2,1)S(1)} %copy-done, f32[512,768]{1,0:T(8,128)} %fusion.61, f32[512,768]{1,0:T(8,128)} %fusion.63, bf16[3,1536,768]{2,1,0:T(8,128)(2,1)} %param.11, bf16[528,1536]{1,0:T(8,128)(2,1)} %copy-done.18, bf16[512,1536]{1,0:T(8,128)(2,1)} %param.10), kind=kOutput, calls=%fused_computation.141 | convolution fusion | flops 2445409792 | bytes 14157824 | tf_op jit(solution)/shard_map/dot_general | solution.py:140
  74.9 4.5 select_select_fusion.2
  91.9 7.4 %all-gather.2.cloned.1.call-done = bf16[8192,256]{1,0:T(8,128)(2,1)} async-done(((bf16[512,256]{1,0:T(8,128)(2,1)}), bf16[8192,256]{1,0:T(8,128)(2,1)}) %all-gather.2.cloned.1.call-update) | async-done | bytes 4194320 | tf_op jit(solution)/shard_map/all_gather | solution.py:192
  99.3 434.7 %while.20 = (s32[]{:T(128)}, f32[512,1]{0,1:T(1,128)S(1)}, f32[512,1]{0,1:T(1,128)S(1)}, f32[512,1,128]{0,2,1:T(8,128)}, s32[]{:T(128)}, /*index=5*/s32[8192]{0:...) while((s32[]{:T(128)}, f32[512,1]{0,1:T(1,128)S(1)}, ...), condition=%wide.region_11.12_spmd, body=%wide.region_4.11_spmd.sunk | while | flops 285161664 | bytes 33061628 | solution.py:205
  112.5 3.9 select_select_fusion.5
  123.9 4.1 fusion.191
  137.8 4.3 select_select_fusion.6
  166.9 3.9 select_select_fusion.5
  178.2 4.1 fusion.191
  192.1 4.3 select_select_fusion.6
  221.2 3.9 select_select_fusion.5
  232.6 4.1 fusion.191
  246.5 4.3 select_select_fusion.6
  275.6 3.9 select_select_fusion.5
  286.9 4.1 fusion.191
  300.8 4.3 select_select_fusion.6
  329.9 3.9 select_select_fusion.5
  341.2 4.1 fusion.191
  355.2 4.3 select_select_fusion.6
  384.3 3.9 select_select_fusion.5
  395.6 4.1 fusion.191
  409.5 4.3 select_select_fusion.6
  438.6 3.9 select_select_fusion.5
  449.9 4.1 fusion.191
  463.8 4.3 select_select_fusion.6
  492.9 3.9 select_select_fusion.5
  504.2 4.1 fusion.191
  518.1 4.3 select_select_fusion.6
  (845 shorter events, 383.3 us)
Async XLA Ops:
  6.5 26.1 %copy-start = (bf16[768,1536]{1,0:T(8,128)(2,1)S(1)}, bf16[768,1536]{1,0:T(8,128)(2,1)}, u32[]{:S(2)}) copy-start(bf16[768,1536]{1,0:T(8,128)(2,1)} %param.12) | copy-start | bytes 7077892
  6.5 92.8 %all-gather.2.cloned.1.call-start = ((), (), s32[]{:S(2)}) async-start(), calls=%async_computation | async-start | bytes 4456448 | tf_op jit(solution)/shard_map/all_gather | solution.py:192
  7.4 6.5 %collective-permute-start = (bf16[8,1536]{1,0:T(8,128)(2,1)S(1)}, bf16[8,1536]{1,0:T(8,128)(2,1)S(1)}, u32[]{:S(2)}, u32[]{:S(2)}) collective-permute-start(bf16[8,1536]{1,0:T(8,128)(2,1)S(1)} %get-tuple-element.461), channel_id=1, source_target_pairs={{0,1},{1,2},{2,3},{3,4},{4,5},{5,6},{6,7},{7,8},{8,9},{9,10},{10,1... | collective-permute-start | bytes 73736 | tf_op jit(solution)/shard_map/ppermute | solution.py:24
  9.4 6.0 %collective-permute-start.1 = (bf16[8,1536]{1,0:T(8,128)(2,1)S(1)}, bf16[8,1536]{1,0:T(8,128)(2,1)S(1)}, u32[]{:S(2)}, u32[]{:S(2)}) collective-permute-start(bf16[8,1536]{1,0:T(8,128)(2,1)S(1)} %get-tuple-element.462), channel_id=1, source_target_pairs={{1,0},{2,1},{3,2},{4,3},{5,4},{6,5},{7,6},{8,7},{9,8},{10,9},{11,1... | collective-permute-start | bytes 73736 | tf_op jit(solution)/shard_map/ppermute | solution.py:25
  23.6 4.8 copy-start.18
  44.2 12.7 %copy-start.16 = (bf16[16,128,128]{2,1,0:T(8,128)(2,1)S(1)}, bf16[16,128,128]{2,1,0:T(8,128)(2,1)}, u32[]{:S(2)}) copy-start(bf16[16,128,128]{2,1,0:T(8,128)(2,1)} %param.15) | copy-start | bytes 1572868
  84.8 4.2 copy-start.17
  84.8 4.2 copy-start.21
  84.8 4.2 copy-start.19
  84.8 4.2 copy-start.20
  123.9 4.7 copy-start.23
  143.6 4.8 copy-start.25
  178.2 4.7 copy-start.23
  196.5 3.7 copy-start.24
  196.5 3.7 copy-start.26
  197.9 4.8 copy-start.25
  232.6 4.7 copy-start.23
  252.2 4.8 copy-start.25
  286.9 4.7 copy-start.23
  305.2 3.7 copy-start.24
  305.2 3.7 copy-start.26
  306.6 4.8 copy-start.25
  341.2 4.7 copy-start.23
  360.9 4.8 copy-start.25
  395.6 4.7 copy-start.23
  413.8 3.7 copy-start.24
  413.8 3.7 copy-start.26
  415.2 4.8 copy-start.25
  449.9 4.7 copy-start.23
  469.6 4.8 copy-start.25
  504.2 4.7 copy-start.23
  523.9 4.8 copy-start.25
  (131 other events, 147.1 us)
Sparse Core Ops, SparseCore 0:
  47.8 51.4 all-gather.1
where the time goes:
time: 549 us; the launch traced here: 543 us
  local copies, waits for them, and re-layouts  273 us (50%)
  other arithmetic  131 us (24%)
  matrix products  107 us (19%)
  between operations  13.6 us (2%)
  waiting for transfers between devices  8.88 us (2%)
  starting transfers between devices  6.45 us (1%)
    eq x289, local copies, waits for them, and re-layouts, tile_bias(): picked_full == code  194 us
    select_n x17, other arithmetic, tile_bias(): jnp.where(picked_full == code, spread_tile.astype(jnp.float32), bias_block)  70.4 us
    dot_general x17, matrix products, block_scores(): jnp.einsum('qhd,khd->qhk', query_heads, key_heads, preferred_element_type...  54.6 us
    convert_element_type x25, local copies, waits for them, and re-layouts, tile_bias(): spread_tile.astype(jnp.float32)  29 us
    dot_general x17, matrix products, absorb(): jnp.einsum('qhk,khd->qhd', probs.astype(jnp.bfloat16), value_heads, prefe...  25.3 us
    select_n x17, local copies, waits for them, and re-layouts, tile_bias(): jnp.where(picked_full == code, spread_tile.astype(jnp.float32), bias_block)  24 us
    convert_element_type x9, other arithmetic, tile_bias(): spread_tile.astype(jnp.float32)  14.6 us
    reduce_sum x9, other arithmetic, absorb(): row_total = row_total + jnp.sum(probs, axis=-1)  12.4 us
  transfers between devices with their start and end apart: 3, of which 2 were waited for; matrix products, arithmetic and copies ran while one was open for 8% of the time, Pallas kernels for 0%

commit v1 on v0

v1 whole, which is shorter than its diff:
```python
import functools
import math

import jax
import jax.numpy as jnp
from jax import lax
from jax.experimental import pallas as pl
from jax.experimental.pallas import tpu as pltpu
from jax.sharding import PartitionSpec as P

HDIM = 128
CONV_DILATION = 8
HALF = 4096
MESH = pl.DeviceIdType.MESH

masked_score = -1e30
norm_eps = 1e-06


def padded(x, axis, width):
    size, length = lax.axis_size(axis), x.shape[0]
    up = [(i, i + 1) for i in range(size - 1)]
    down = [(j, i) for i, j in up]
    before = lax.ppermute(x[length - width :], axis, up)
    after = lax.ppermute(x[:width], axis, down)
    return jnp.concatenate([before, x, after], axis=0)


class Place:
    def __init__(self, count, columns, reach):
        self.count = count
        self.columns = columns
        self.plane = 2 * columns
        self.planes = count // self.plane
        self.reach = reach
        self.far = -(-reach // self.plane)
        self.steps = (2 * self.far + 1) * columns
        me = lax.axis_index("seq")
        self.me = me
        self.z = me // self.plane
        self.y = (me % self.plane) // 2
        self.core = me % 2

    def index(self, z, y, core):
        return z * self.plane + y * 2 + core

    def step(self, k):
        kk = jnp.maximum(k - self.columns, 0)
        rem = kk % (2 * self.columns)
        late = k >= self.columns
        dz = jnp.where(late, (kk // (2 * self.columns) + 1) * (2 * (rem % 2) - 1), 0)
        flip = jnp.where(late, rem // 2, k)
        return dz, flip

    def needs(self, source, target):
        return jnp.abs(source - target) <= self.reach


def block_moves(place, kvbuf, send_sem, recv_sem, dz, flip, half, rows):
    z, y, core = place.z, place.y, place.core
    source_z = z + dz
    source = place.index(source_z, (y + flip) % 2 if place.columns == 2 else y, core)
    held = (source_z >= 0) & (source_z < place.planes) & place.needs(source, place.me)
    piece = kvbuf.at[source, pl.ds(half * rows, rows)]
    slot = (dz + place.far) * place.columns + flip
    edge = (source_z == 0) | (source_z == place.planes - 1)
    away = jnp.abs(dz)

    def along_z(distance):
        return (distance == 1) & (edge | (half == 1))

    def copy(kind, target):
        return pltpu.make_async_remote_copy(
            src_ref=piece,
            dst_ref=piece,
            send_sem=send_sem.at[kind, slot, half],
            recv_sem=recv_sem.at[source, half],
            device_id={"seq": target},
            device_id_type=MESH,
        )

    moves = []
    for kind, turn in ((0, 1), (1, -1)):
        target = jnp.clip(place.index(z + turn, y, core), 0, place.count - 1)
        go = held & (z + turn >= 0) & (z + turn < place.planes)
        go = go & (dz * turn <= 0) & (away + 1 <= place.far) & place.needs(source, target)
        go = go & ((flip == 0) | along_z(away + 1))
        moves.append((go, copy(kind, target)))
    if place.columns == 2:
        target = place.index(z, 1 - y, core)
        go = held & (flip == 0) & ((dz == 0) | jnp.logical_not(along_z(away)))
        moves.append((go & place.needs(source, target), copy(2, target)))
    target = place.index(z, y, 1 - core)
    moves.append((held & place.needs(source, target), copy(3, target)))
    return source, held, moves


def attention_kernel(
    columns,
    count,
    q_ref,
    kv_ref,
    table_ref,
    codes_ref,
    valid_ref,
    out_ref,
    kvbuf,
    peak,
    total,
    weighted,
    send_sem,
    recv_sem,
):
    rows = q_ref.shape[0]
    half_rows = rows // 2
    tile = table_ref.shape[1]
    tiles = rows // tile
    offsets = codes_ref.shape[1]
    place = Place(count, columns, HALF // rows)
    me, z, y, core = place.me, place.z, place.y, place.core
    scale = 1.0 / math.sqrt(HDIM)

    barrier = pltpu.get_barrier_semaphore()
    greeted = [(jnp.bool_(True), place.index(z, y, 1 - core))]
    if columns == 2:
        greeted.append((jnp.bool_(True), place.index(z, 1 - y, core)))
    for turn in (1, -1):
        ok = (z + turn >= 0) & (z + turn < place.planes)
        greeted.append((ok, jnp.clip(place.index(z + turn, y, core), 0, count - 1)))
    for ok, target in greeted:

        @pl.when(ok)
        def _():
            pl.semaphore_signal(barrier, inc=1, device_id={"seq": target}, device_id_type=MESH)

    pl.semaphore_wait(barrier, sum(ok.astype(jnp.int32) for ok, _target in greeted))

    kvbuf[me] = kv_ref[...]
    peak[...] = jnp.full(peak.shape, masked_score, jnp.float32)
    total[...] = jnp.zeros(total.shape, jnp.float32)
    weighted[...] = jnp.zeros(weighted.shape, jnp.float32)

    def absorb(source, special):
        delta = source - me
        keys = kvbuf[source, :, :HDIM]
        values = kvbuf[source, :, HDIM:]
        raw = lax.dot_general(
            q_ref[...], keys, (((1,), (1,)), ((), ())), preferred_element_type=jnp.float32
        )
        bias = []
        for i in range(tiles):
            line = []
            for j in range(tiles):
                offset = jnp.clip(delta * tiles + (j - i) + offsets // 2, 0, offsets - 1)
                line.append(table_ref[codes_ref[i, offset]])
            bias.append(jnp.concatenate(line, axis=1))
        scores = raw * scale + jnp.concatenate(bias, axis=0)
        if special:
            row = lax.broadcasted_iota(jnp.int32, (rows, rows), 0)
            col = lax.broadcasted_iota(jnp.int32, (rows, rows), 1)
            apart = delta * rows + col - row
            kept = (apart == 0) | ((jnp.abs(apart) <= HALF) & (valid_ref[source] >= 0.0))
            scores = jnp.where(kept, scores, masked_score)
        else:
            scores = scores + valid_ref[source]
        old = peak[...]
        new = jnp.maximum(old, jnp.max(scores, axis=1, keepdims=True))
        probs = jnp.exp(scores - new)
        shrink = jnp.exp(old - new)
        peak[...] = new
        total[...] = total[...] * shrink + jnp.sum(probs, axis=1, keepdims=True)
        weighted[...] = weighted[...] * shrink + jnp.dot(
            probs.astype(jnp.bfloat16), values, preferred_element_type=jnp.float32
        )

    def absorb_block(source):
        apart = jnp.abs(source - me)
        special = (apart == 0) | (apart == place.reach)

        @pl.when(special)
        def _():
            absorb(source, True)

        @pl.when(jnp.logical_not(special))
        def _():
            absorb(source, False)

    def arrived(source, half):
        piece = kvbuf.at[source, pl.ds(half * half_rows, half_rows)]
        pltpu.make_async_copy(piece, piece, recv_sem.at[source, half]).wait()

    def moves_of(k, half):
        dz, flip = place.step(k)
        return block_moves(place, kvbuf, send_sem, recv_sem, dz, flip, half, half_rows)

    def turn_of(k, carry):
        for half in range(2):
            source, held, moves = moves_of(k, half)
            held = held & (k < place.steps)

            @pl.when(held & (k > 0))
            def _():
                arrived(source, half)

            for go, copy in moves:

                @pl.when(go & held)
                def _():
                    copy.start()

        dz, flip = place.step(jnp.maximum(k - 1, 0))
        other_z = z + dz
        other = place.index(other_z, (y + flip) % 2 if columns == 2 else y, 1 - core)
        take = (k > 0) & (other_z >= 0) & (other_z < place.planes) & place.needs(other, me)

        @pl.when(held)
        def _():
            absorb_block(source)

        @pl.when(take)
        def _():
            arrived(other, 0)
            arrived(other, 1)
            absorb_block(other)

        return carry

    lax.fori_loop(0, place.steps + 1, turn_of, 0)
    out_ref[...] = (weighted[...] / total[...]).astype(out_ref.dtype)

    def drain(k, carry):
        for half in range(2):
            _source, _held, moves = moves_of(k, half)
            for go, copy in moves:

                @pl.when(go)
                def _():
                    copy.wait_send()

        return carry

    lax.fori_loop(0, place.steps, drain, 0)


def attention(columns, queries, keyval, table, codes, valid):
    rows = queries.shape[0]
    count = lax.axis_size("seq")
    plane = 2 * columns
    far = -(-(HALF // rows) // plane)
    vmem = pl.BlockSpec(memory_space=pltpu.VMEM)
    smem = pl.BlockSpec(memory_space=pltpu.SMEM)
    return pl.pallas_call(
        functools.partial(attention_kernel, columns, count),
        out_shape=jax.ShapeDtypeStruct((rows, HDIM), jnp.bfloat16),
        in_specs=[vmem, vmem, vmem, smem, vmem],
        out_specs=vmem,
        scratch_shapes=[
            pltpu.VMEM((count, rows, 2 * HDIM), jnp.bfloat16),
            pltpu.VMEM((rows, 1), jnp.float32),
            pltpu.VMEM((rows, 1), jnp.float32),
            pltpu.VMEM((rows, HDIM), jnp.float32),
            pltpu.SemaphoreType.DMA((4, (2 * far + 1) * columns, 2)),
            pltpu.SemaphoreType.DMA((count, 2)),
        ],
        compiler_params=pltpu.CompilerParams(
            collective_id=0, has_side_effects=True, vmem_limit_bytes=48 * 1024 * 1024
        ),
        cost_estimate=pl.CostEstimate(
            flops=4 * rows * HDIM * 2 * HALF,
            bytes_accessed=4 * 1024 * 1024,
            transcendentals=rows * 2 * HALF,
        ),
    )(queries, keyval, table, codes, valid)


def per_device(
    columns,
    activations,
    dilated_tap_weight,
    conv_mix,
    w_query,
    w_keyval,
    contact_tiles,
    tile_codes,
    bin_valid,
):
    rows = activations.shape[0]
    count = lax.axis_size("seq")
    border_padded = padded(activations, "seq", CONV_DILATION)
    lifted = jax.nn.gelu(border_padded.astype(jnp.float32), approximate=False).astype(jnp.bfloat16)
    conv_sum = jnp.zeros((rows, dilated_tap_weight.shape[2]), jnp.float32)
    for tap in range(3):
        conv_sum = conv_sum + jnp.dot(
            lifted[tap * CONV_DILATION : tap * CONV_DILATION + rows],
            dilated_tap_weight[tap],
            preferred_element_type=jnp.float32,
        )
    squeezed = jax.nn.gelu(conv_sum, approximate=False).astype(jnp.bfloat16)
    mixed_rows = activations.astype(jnp.float32) + jnp.dot(
        squeezed, conv_mix, preferred_element_type=jnp.float32
    )
    normed = (
        mixed_rows * lax.rsqrt(jnp.mean(mixed_rows * mixed_rows, axis=-1, keepdims=True) + norm_eps)
    ).astype(jnp.bfloat16)
    queries = jnp.dot(normed, w_query, preferred_element_type=jnp.float32).astype(jnp.bfloat16)
    keyval = jnp.dot(normed, w_keyval, preferred_element_type=jnp.float32).astype(jnp.bfloat16)
    valid = jnp.where(bin_valid == 1, 0.0, masked_score).astype(jnp.float32)
    valid = valid.reshape(count, 1, rows)
    table = contact_tiles.astype(jnp.float32)
    return attention(columns, queries, keyval, table, tile_codes, valid)


def columns_of(mesh):
    along = mesh.devices.reshape(-1, mesh.shape["seq"])[0]
    first = along[0]
    if not hasattr(first, "coords"):
        return 2 if mesh.shape["seq"] == 16 else 1
    return sum(d.coords[2] == first.coords[2] for d in along) // 2


def solution(mesh):
    in_specs = (P(("grp", "seq"), None), P(), P(), P(), P(), P(), P(("grp", "seq"), None), P("grp"))
    out_specs = P(("grp", "seq"), None)
    return jax.shard_map(
        functools.partial(per_device, columns_of(mesh)),
        mesh=mesh,
        in_specs=in_specs,
        out_specs=out_specs,
        check_vma=False,
    )
```

time: 549 us -> 79.4 us (0.14)
  local copies, waits for them, and re-layouts: 273 us -> 1.92 us
  other arithmetic: 131 us -> 9.05 us
  matrix products: 107 us -> 24 us
  Pallas kernels: 0 us -> 36.3 us
  between operations: 13.6 us -> 0.09 us
  waiting for transfers between devices: 8.88 us -> 0.01 us
    eq x289 -> x0, local copies, waits for them, and re-layouts: 194 us -> none  [tile_bias(): picked_full == code]
    dot_general x36 -> x2, matrix products: 89 us -> 9.02 us  [per_device(): jnp.dot(lifted[tap * CONV_DILATION:tap * CONV_DILATION + rows], dilated_t...]
    select_n x17 -> x1, other arithmetic: 70.4 us -> 0.76 us  [per_device(): valid = jnp.where(bin_valid == 1, 0.0, masked_score).astype(jnp.float32)]
    pallas_call x0 -> x1, Pallas kernels: none -> 36.3 us  [attention(): pl.pallas_call(functools.partial(attention_kernel, columns, count), out_s...]
    convert_element_type x25 -> x0, local copies, waits for them, and re-layouts: 29 us -> none  [tile_bias(): spread_tile.astype(jnp.float32)]
    select_n x17 -> x0, local copies, waits for them, and re-layouts: 24 us -> none  [tile_bias(): jnp.where(picked_full == code, spread_tile.astype(jnp.float32), bias_block)]
    eq x26 -> x0, other arithmetic: 21.5 us -> none  [the longest x9 11.8 us: block_scores(): valid_keys[None, :] == 1]
    reduce_sum x18 -> x0, other arithmetic: 14.9 us -> none  [the longest x9 12.4 us: absorb(): row_total = row_total + jnp.sum(probs, axis=-1)]
  transfers between devices with their start and end apart: 3 -> 2, of which waited for: 2 -> 0; matrix products, arithmetic and copies ran while one was open for 8% -> 2% of each run, Pallas kernels for 0% -> 0%
where the time goes in v1:
time: 79.4 us; the launch traced here: 77.9 us
  Pallas kernels  36.3 us (46%)
  matrix products  24 us (30%)
  other arithmetic  9.05 us (11%)
  starting transfers between devices  6.58 us (8%)
  local copies, waits for them, and re-layouts  1.92 us (2%)
    pallas_call x1, Pallas kernels, attention(): pl.pallas_call(functools.partial(attention_kernel, columns, count), out_s...  36.3 us
    dot_general x1, matrix products, per_device(): jnp.dot(squeezed, conv_mix, preferred_element_type=jnp.float32)  11.5 us
    dot_general x2, matrix products, per_device(): jnp.dot(lifted[tap * CONV_DILATION:tap * CONV_DILATION + rows], dilated_t...  9.02 us
    convert_element_type x1, other arithmetic, per_device(): jax.nn.gelu(border_padded.astype(jnp.float32), approximate=False)  7.15 us
    ppermute x1, starting transfers between devices, padded(): after = lax.ppermute(x[:width], axis, down)  4.54 us
    dot_general x1, matrix products, per_device(): jnp.dot(normed, w_keyval, preferred_element_type=jnp.float32)  2.84 us
    ppermute x1, starting transfers between devices, padded(): before = lax.ppermute(x[length - width:], axis, up)  2.04 us
  transfers between devices with their start and end apart: 2, of which 0 were waited for; matrix products, arithmetic and copies ran while one was open for 2% of the time, Pallas kernels for 0%

profile of v1, /device:TPU:18, one launch (start us, length us, event | category | flops | bytes accessed | tf_op | source)
XLA Modules:
  0.0 77.9 jit_solution(2167160334426198103)
XLA Ops:
  0.0 0.0 copy-start
  0.0 0.0 copy-start.3
  0.0 0.9 %fusion.122 = (bf16[8,1536]{1,0:T(8,128)(2,1)S(1)}, bf16[8,1536]{1,0:T(8,128)(2,1)S(1)}) fusion(bf16[512,1536]{1,0:T(8,128)(2,1)} %param.8), kind=kLoop, calls=%fused_computation.133 | loop fusion | bytes 98304 | tf_op jit(solution)/shard_map/slice | solution.py:24
  0.9 2.0 %collective-permute-start = (bf16[8,1536]{1,0:T(8,128)(2,1)S(1)}, bf16[8,1536]{1,0:T(8,128)(2,1)S(1)}, u32[]{:S(2)}, u32[]{:S(2)}) collective-permute-start(bf16[8,1536]{1,0:T(8,128)(2,1)S(1)} %get-tuple-element.5), channel_id=1, source_target_pairs={{0,1},{1,2},{2,3},{3,4},{4,5},{5,6},{6,7},{7,8},{8,9},{9,10},{10,1... | collective-permute-start | bytes 73736 | tf_op jit(solution)/shard_map/ppermute | solution.py:24
  3.0 4.5 %collective-permute-start.1 = (bf16[8,1536]{1,0:T(8,128)(2,1)S(1)}, bf16[8,1536]{1,0:T(8,128)(2,1)S(1)}, u32[]{:S(2)}, u32[]{:S(2)}) collective-permute-start(bf16[8,1536]{1,0:T(8,128)(2,1)S(1)} %get-tuple-element.6), channel_id=1, source_target_pairs={{1,0},{2,1},{3,2},{4,3},{5,4},{6,5},{7,6},{8,7},{9,8},{10,9},{11,1... | collective-permute-start | bytes 73736 | tf_op jit(solution)/shard_map/ppermute | solution.py:25
  7.5 0.8 compare_select_fusion
  8.3 1.1 %convert_element_type.31.table_ref = f32[16,128,128]{2,1,0:T(8,128)S(1)} convert(bf16[16,128,128]{2,1,0:T(8,128)(2,1)} %param.13) | non-fusion elementwise | flops 262144 | bytes 1572864 | tf_op jit(solution)/shard_map/convert_element_type | solution.py:309
  9.4 0.0 collective-permute-done
  9.4 0.0 collective-permute-done.1
  9.4 0.0 copy-done.3
  9.5 7.2 %fusion.1 = bf16[528,1536]{1,0:T(8,128)(2,1)S(1)} fusion(bf16[8,1536]{1,0:T(8,128)(2,1)S(1)} %collective-permute-done.1, bf16[512,1536]{1,0:T(8,128)(2,1)S(1)} %copy-done.3, bf16[8,1536]{1,0:T(8,128)(2,1)S(1)} %collective-permute-done), kind=kLoop, calls=%fused_computation.4 | loop fusion | flops 57581568 | bytes 3244032 | tf_op jit(solution)/shard_map/convert_element_type | solution.py:290
  16.6 0.0 copy-start.4
  16.6 4.8 %fusion.31 = f32[512,768]{1,0:T(8,128)} fusion(bf16[3,1536,768]{2,1,0:T(8,128)(2,1)} %param.9, bf16[528,1536]{1,0:T(8,128)(2,1)S(1)} %fusion.1), kind=kOutput, calls=%fused_computation.38 | convolution fusion | flops 1207959552 | bytes 5505024 | tf_op jit(solution)/shard_map/dot_general | solution.py:293
  21.4 0.0 copy-done.4
  21.4 4.2 %fusion.33 = f32[512,768]{1,0:T(8,128)} fusion(bf16[3,1536,768]{2,1,0:T(8,128)(2,1)} %param.9, bf16[528,1536]{1,0:T(8,128)(2,1)S(1)} %fusion.1), kind=kOutput, calls=%fused_computation.40 | convolution fusion | flops 1207959552 | bytes 5505024 | tf_op jit(solution)/shard_map/dot_general | solution.py:293
  25.6 0.0 copy-done
  25.7 11.5 %multiply_reduce_fusion = (f32[512]{0:T(512)S(1)}, f32[512,1536]{1,0:T(8,128)}) fusion(bf16[768,1536]{1,0:T(8,128)(2,1)S(1)} %copy-done, f32[512,768]{1,0:T(8,128)} %fusion.31, f32[512,768]{1,0:T(8,128)} %fusion.33, bf16[3,1536,768]{2,1,0:T(8,128)(2,1)} %param.9, bf16[528,1536]{1,0:T(8,128)(2,1)} %copy-done.4, bf16[512,1536]{1,0:T(8,128)(2,1)} %param.8), kind=kOutput, calls=%fused_computation.36 | convolution fusion | flops 2445409792 | bytes 14157824 | tf_op jit(solution)/shard_map/dot_general | solution.py:299
  37.2 0.0 copy-start.2
  37.2 0.0 copy-start.5
  37.2 2.8 %convolution_convert_fusion.kv_ref = bf16[512,256]{1,0:T(8,128)(2,1)S(1)} fusion(bf16[1536,256]{1,0:T(8,128)(2,1)} %param.12, f32[512,1536]{1,0:T(8,128)} %get-tuple-element.8, f32[512]{0:T(512)S(1)} %add_rsqrt_fusion), kind=kOutput, calls=%fused_computation.69 | convolution fusion | flops 404357120 | bytes 4196352 | tf_op jit(solution)/shard_map/dot_general | solution.py:306
  40.0 0.2 copy-done.2
  40.3 0.1 copy-done.5
  40.3 0.0 copy-start.1
  40.3 0.6 convolution_convert_fusion.1.q_ref
  40.9 0.1 copy-done.1
  41.0 36.3 %shard_map.82 = bf16[512,128]{1,0:T(8,128)(2,1)S(1)} custom-call(bf16[512,128]{1,0:T(8,128)(2,1)S(1)} %convolution_convert_fusion.1.q_ref, bf16[512,256]{1,0:T(8,128)(2,1)S(1)} %convolution_convert_fusion.kv_ref, f32[16,128,128]{2,1,0:T(8,128)S(1)} %convert_element_type.31.table_ref, s32[4,65]{1,0:T(4,128)S(1)} %copy-done.1, f32[16,1,512]{2,1,0:T(1,128)S(1)} %bitcast.19), custom_call_target="tpu_custom_call" | custom-call | flops 2147483648 | bytes 4194304 | tf_op jit(solution)/shard_map/pallas_call | solution.py:252
  77.3 0.7 copy.10
  (1 shorter events, 0.0 us)
Async XLA Ops:
  0.0 25.7 %copy-start = (bf16[768,1536]{1,0:T(8,128)(2,1)S(1)}, bf16[768,1536]{1,0:T(8,128)(2,1)}, u32[]{:S(2)}) copy-start(bf16[768,1536]{1,0:T(8,128)(2,1)} %param.10) | copy-start | bytes 7077892
  0.0 9.4 %copy-start.3 = (bf16[512,1536]{1,0:T(8,128)(2,1)S(1)}, bf16[512,1536]{1,0:T(8,128)(2,1)}, u32[]{:S(2)}) copy-start(bf16[512,1536]{1,0:T(8,128)(2,1)} %param.8) | copy-start | bytes 4718596
  0.9 8.5 %collective-permute-start = (bf16[8,1536]{1,0:T(8,128)(2,1)S(1)}, bf16[8,1536]{1,0:T(8,128)(2,1)S(1)}, u32[]{:S(2)}, u32[]{:S(2)}) collective-permute-start(bf16[8,1536]{1,0:T(8,128)(2,1)S(1)} %get-tuple-element.5), channel_id=1, source_target_pairs={{0,1},{1,2},{2,3},{3,4},{4,5},{5,6},{6,7},{7,8},{8,9},{9,10},{10,1... | collective-permute-start | bytes 73736 | tf_op jit(solution)/shard_map/ppermute | solution.py:24
  3.0 6.5 %collective-permute-start.1 = (bf16[8,1536]{1,0:T(8,128)(2,1)S(1)}, bf16[8,1536]{1,0:T(8,128)(2,1)S(1)}, u32[]{:S(2)}, u32[]{:S(2)}) collective-permute-start(bf16[8,1536]{1,0:T(8,128)(2,1)S(1)} %get-tuple-element.6), channel_id=1, source_target_pairs={{1,0},{2,1},{3,2},{4,3},{5,4},{6,5},{7,6},{8,7},{9,8},{10,9},{11,1... | collective-permute-start | bytes 73736 | tf_op jit(solution)/shard_map/ppermute | solution.py:25
  16.6 4.8 %copy-start.4 = (bf16[528,1536]{1,0:T(8,128)(2,1)}, bf16[528,1536]{1,0:T(8,128)(2,1)S(1)}, u32[]{:S(2)}) copy-start(bf16[528,1536]{1,0:T(8,128)(2,1)S(1)} %fusion.1) | copy-start | bytes 4866052
  37.2 3.1 %copy-start.2 = (f32[512,1536]{1,0:T(8,128)S(1)}, f32[512,1536]{1,0:T(8,128)}, u32[]{:S(2)}) copy-start(f32[512,1536]{1,0:T(8,128)} %get-tuple-element.8) | copy-start | bytes 9437188
  37.2 3.1 %copy-start.5 = (bf16[1536,128]{1,0:T(8,128)(2,1)S(1)}, bf16[1536,128]{1,0:T(8,128)(2,1)}, u32[]{:S(2)}) copy-start(bf16[1536,128]{1,0:T(8,128)(2,1)} %param.11) | copy-start | bytes 1179652
  40.3 0.7 copy-start.1

commit v2 on v1

v2 whole, which is shorter than its diff:
```python
import functools
import math

import jax
import jax.numpy as jnp
from jax import lax
from jax.experimental import pallas as pl
from jax.experimental.pallas import tpu as pltpu
from jax.sharding import PartitionSpec as P

HDIM = 128
CONV_DILATION = 8
HALF = 4096
MESH = pl.DeviceIdType.MESH

masked_score = -1e30
norm_eps = 1e-06
LOG2E = math.log2(math.e)


class Place:
    def __init__(self, count, columns, reach):
        self.count = count
        self.columns = columns
        self.plane = 2 * columns
        self.planes = count // self.plane
        self.reach = reach
        self.far = -(-reach // self.plane)
        self.steps = (2 * self.far + 1) * columns
        me = lax.axis_index("seq")
        self.me = me
        self.z = me // self.plane
        self.y = (me % self.plane) // 2
        self.core = me % 2

    def index(self, z, y, core):
        return z * self.plane + y * 2 + core

    def step(self, k):
        kk = jnp.maximum(k - self.columns, 0)
        rem = kk % (2 * self.columns)
        late = k >= self.columns
        dz = jnp.where(late, (kk // (2 * self.columns) + 1) * (2 * (rem % 2) - 1), 0)
        flip = jnp.where(late, rem // 2, k)
        return dz, flip

    def needs(self, source, target):
        return jnp.abs(source - target) <= self.reach


def block_moves(place, kvbuf, send_sem, recv_sem, dz, flip, half, rows):
    z, y, core = place.z, place.y, place.core
    source_z = z + dz
    source = place.index(source_z, (y + flip) % 2 if place.columns == 2 else y, core)
    held = (source_z >= 0) & (source_z < place.planes) & place.needs(source, place.me)
    piece = kvbuf.at[source, pl.ds(half * rows, rows)]
    slot = (dz + place.far) * place.columns + flip
    edge = (source_z == 0) | (source_z == place.planes - 1)
    away = jnp.abs(dz)

    def along_z(distance):
        return (distance == 1) & (edge | (half == 1))

    def copy(kind, target):
        return pltpu.make_async_remote_copy(
            src_ref=piece,
            dst_ref=piece,
            send_sem=send_sem.at[kind, slot, half],
            recv_sem=recv_sem.at[source, half],
            device_id={"seq": target},
            device_id_type=MESH,
        )

    moves = []
    for kind, turn in ((0, 1), (1, -1)):
        target = jnp.clip(place.index(z + turn, y, core), 0, place.count - 1)
        go = held & (z + turn >= 0) & (z + turn < place.planes)
        go = go & (dz * turn <= 0) & (away + 1 <= place.far) & place.needs(source, target)
        go = go & ((flip == 0) | along_z(away + 1))
        moves.append((go, copy(kind, target)))
    if place.columns == 2:
        target = place.index(z, 1 - y, core)
        go = held & (flip == 0) & ((dz == 0) | jnp.logical_not(along_z(away)))
        moves.append((go & place.needs(source, target), copy(2, target)))
    target = place.index(z, y, 1 - core)
    moves.append((held & place.needs(source, target), copy(3, target)))
    return source, held, moves


def gelu(v):
    return 0.5 * v * (1.0 + lax.erf(v * math.sqrt(0.5)))


def layer_kernel(
    columns,
    count,
    act_hbm,
    taps_hbm,
    mix_hbm,
    wq_hbm,
    wkv_hbm,
    tiles_ref,
    codes_ref,
    valid_ref,
    out_ref,
    act,
    taps,
    mix,
    wq,
    wkv,
    halo,
    lifted,
    squeezed,
    mixed,
    normed,
    table,
    queries,
    scores_buf,
    probs_buf,
    kvbuf,
    peak,
    total,
    weighted,
    load_sem,
    halo_send,
    halo_recv,
    send_sem,
    recv_sem,
):
    rows, channels = act.shape
    hidden = mix.shape[0]
    half_rows = rows // 2
    tile = table.shape[1]
    tiles = rows // tile
    offsets = codes_ref.shape[1]
    edge = halo.shape[1]
    place = Place(count, columns, HALF // rows)
    me, z, y, core = place.me, place.z, place.y, place.core

    loads = [
        pltpu.make_async_copy(act_hbm, act, load_sem.at[0]),
        pltpu.make_async_copy(taps_hbm.at[0], taps.at[0], load_sem.at[1]),
        pltpu.make_async_copy(taps_hbm.at[1], taps.at[1], load_sem.at[2]),
        pltpu.make_async_copy(taps_hbm.at[2], taps.at[2], load_sem.at[3]),
        pltpu.make_async_copy(mix_hbm, mix, load_sem.at[4]),
        pltpu.make_async_copy(wq_hbm, wq, load_sem.at[5]),
        pltpu.make_async_copy(wkv_hbm, wkv, load_sem.at[6]),
    ]
    for load in loads:
        load.start()

    barrier = pltpu.get_barrier_semaphore()
    greeted = [(jnp.bool_(True), place.index(z, y, 1 - core))]
    if columns == 2:
        greeted.append((jnp.bool_(True), place.index(z, 1 - y, core)))
    for turn in (1, -1):
        ok = (z + turn >= 0) & (z + turn < place.planes)
        greeted.append((ok, jnp.clip(place.index(z + turn, y, core), 0, count - 1)))
    beyond = me + 2 * core - 1
    greeted.append(((beyond >= 0) & (beyond < count), jnp.clip(beyond, 0, count - 1)))
    for ok, target in greeted:

        @pl.when(ok)
        def _():
            pl.semaphore_signal(barrier, inc=1, device_id={"seq": target}, device_id_type=MESH)

    loads[0].wait()
    pl.semaphore_wait(barrier, sum(ok.astype(jnp.int32) for ok, _target in greeted))

    has_next = me + 1 < count
    has_prev = me > 0
    to_next = pltpu.make_async_remote_copy(
        src_ref=act.at[pl.ds(rows - edge, edge)],
        dst_ref=halo.at[0],
        send_sem=halo_send.at[0],
        recv_sem=halo_recv.at[0],
        device_id={"seq": jnp.minimum(me + 1, count - 1)},
        device_id_type=MESH,
    )
    to_prev = pltpu.make_async_remote_copy(
        src_ref=act.at[pl.ds(0, edge)],
        dst_ref=halo.at[1],
        send_sem=halo_send.at[1],
        recv_sem=halo_recv.at[1],
        device_id={"seq": jnp.maximum(me - 1, 0)},
        device_id_type=MESH,
    )

    @pl.when(has_next)
    def _():
        to_next.start()

    @pl.when(has_prev)
    def _():
        to_prev.start()

    table[...] = tiles_ref[...].astype(jnp.float32) * LOG2E
    peak[...] = jnp.full(peak.shape, masked_score, jnp.float32)
    total[...] = jnp.zeros(total.shape, jnp.float32)
    weighted[...] = jnp.zeros(weighted.shape, jnp.float32)

    def lift(strip, carry):
        at = pl.multiple_of(strip * edge, edge)
        lifted[pl.ds(at + edge, edge)] = gelu(act[pl.ds(at, edge)].astype(jnp.float32)).astype(
            jnp.bfloat16
        )
        return carry

    lax.fori_loop(0, rows // edge, lift, 0)

    for side, there, copy in ((0, has_prev, to_next), (1, has_next, to_prev)):
        at = side * (rows + edge)

        @pl.when(there)
        def _():
            copy.wait_recv()
            lifted[at : at + edge] = gelu(halo[side].astype(jnp.float32)).astype(jnp.bfloat16)

        @pl.when(jnp.logical_not(there))
        def _():
            lifted[at : at + edge] = jnp.zeros((edge, channels), jnp.bfloat16)

    def moves_of(k, half):
        dz, flip = place.step(k)
        return block_moves(place, kvbuf, send_sem, recv_sem, dz, flip, half, half_rows)

    def hand_on(held, moves):
        for go, copy in moves:

            @pl.when(go & held)
            def _():
                copy.start()

    for load in loads[1:]:
        load.wait()

    wide = 256
    shift = CONV_DILATION

    def front(half, carry):
        at = pl.multiple_of(half * half_rows, half_rows)
        tall = half_rows + edge
        for n in range(0, hidden, wide):
            low = jnp.dot(
                lifted[pl.ds(at, tall)],
                taps[0, :, n : n + wide],
                preferred_element_type=jnp.float32,
            )
            mid = jnp.dot(
                lifted[pl.ds(at + edge, half_rows)],
                taps[1, :, n : n + wide],
                preferred_element_type=jnp.float32,
            )
            high = jnp.dot(
                lifted[pl.ds(at + edge, tall)],
                taps[2, :, n : n + wide],
                preferred_element_type=jnp.float32,
            )
            conv = low[edge - shift : edge - shift + half_rows] + mid
            conv = conv + high[shift : shift + half_rows]
            squeezed[:, n : n + wide] = gelu(conv).astype(jnp.bfloat16)
        square = jnp.zeros((half_rows, 128), jnp.float32)
        for n in range(0, channels, wide):
            part = act[pl.ds(at, half_rows), n : n + wide].astype(jnp.float32) + jnp.dot(
                squeezed[...], mix[:, n : n + wide], preferred_element_type=jnp.float32
            )
            mixed[:, n : n + wide] = part
            for m in range(0, wide, 128):
                square = square + part[:, m : m + 128] * part[:, m : m + 128]
        mean = jnp.sum(square, axis=1, keepdims=True) * (1.0 / channels)
        factor = lax.rsqrt(mean + norm_eps)
        for n in range(0, channels, wide):
            normed[:, n : n + wide] = (mixed[:, n : n + wide] * factor).astype(jnp.bfloat16)
        keyval = jnp.dot(normed[...], wkv[...], preferred_element_type=jnp.float32)
        kvbuf[me, pl.ds(at, half_rows)] = keyval.astype(jnp.bfloat16)
        _source, held, moves = moves_of(0, half)
        hand_on(held, moves)
        query = jnp.dot(normed[...], wq[...], preferred_element_type=jnp.float32)
        queries[pl.ds(at, half_rows)] = (query * (LOG2E / math.sqrt(HDIM))).astype(jnp.bfloat16)
        return carry

    lax.fori_loop(0, 2, front, 0)

    strip_rows = 32

    def absorb(source, special):
        delta = source - me
        scores_buf[...] = lax.dot_general(
            queries[...],
            kvbuf[source, :, :HDIM],
            (((1,), (1,)), ((), ())),
            preferred_element_type=jnp.float32,
        )
        shrinks = []
        for i in range(tiles):
            codes = []
            for j in range(tiles):
                offset = jnp.clip(delta * tiles + (j - i) + offsets // 2, 0, offsets - 1)
                codes.append(codes_ref[i, offset])
            for r in range(0, tile, strip_rows):
                at = i * tile + r
                bias = jnp.concatenate(
                    [table[code, r : r + strip_rows] for code in codes], axis=1
                )
                scores = scores_buf[at : at + strip_rows] + bias
                if special:
                    row = lax.broadcasted_iota(jnp.int32, (strip_rows, rows), 0) + at
                    col = lax.broadcasted_iota(jnp.int32, (strip_rows, rows), 1)
                    apart = delta * rows + col - row
                    kept = (jnp.abs(apart) <= HALF) & (valid_ref[source] >= 0.0)
                    scores = jnp.where((apart == 0) | kept, scores, masked_score)
                else:
                    scores = scores + valid_ref[source]
                old = peak[at : at + strip_rows]
                new = jnp.maximum(old, jnp.max(scores, axis=1, keepdims=True))
                probs = jnp.exp2(scores - new)
                shrink = jnp.exp2(old - new)
                peak[at : at + strip_rows] = new
                total[at : at + strip_rows] = total[at : at + strip_rows] * shrink + jnp.sum(
                    probs, axis=1, keepdims=True
                )
                weighted[at : at + strip_rows] = weighted[at : at + strip_rows] * shrink
                probs_buf[at : at + strip_rows] = probs.astype(jnp.bfloat16)
        weighted[...] += jnp.dot(
            probs_buf[...], kvbuf[source, :, HDIM:], preferred_element_type=jnp.float32
        )

    def absorb_block(source):
        apart = jnp.abs(source - me)
        special = (apart == 0) | (apart == place.reach)

        @pl.when(special)
        def _():
            absorb(source, True)

        @pl.when(jnp.logical_not(special))
        def _():
            absorb(source, False)

    def arrived(source, half):
        piece = kvbuf.at[source, pl.ds(half * half_rows, half_rows)]
        pltpu.make_async_copy(piece, piece, recv_sem.at[source, half]).wait()

    def turn_of(k, carry):
        for half in range(2):
            source, held, moves = moves_of(k, half)
            held = held & (k < place.steps)

            @pl.when(held & (k > 0))
            def _():
                arrived(source, half)

            hand_on(held & (k > 0), moves)

        dz, flip = place.step(jnp.maximum(k - 1, 0))
        other_z = z + dz
        other = place.index(other_z, (y + flip) % 2 if columns == 2 else y, 1 - core)
        take = (k > 0) & (other_z >= 0) & (other_z < place.planes) & place.needs(other, me)

        @pl.when(held)
        def _():
            absorb_block(source)

        @pl.when(take)
        def _():
            arrived(other, 0)
            arrived(other, 1)
            absorb_block(other)

        return carry

    lax.fori_loop(0, place.steps + 1, turn_of, 0)
    out_ref[...] = (weighted[...] / total[...]).astype(out_ref.dtype)

    def drain(k, carry):
        for half in range(2):
            _source, _held, moves = moves_of(k, half)
            for go, copy in moves:

                @pl.when(go)
                def _():
                    copy.wait_send()

        return carry

    lax.fori_loop(0, place.steps, drain, 0)

    @pl.when(has_next)
    def _():
        to_next.wait_send()

    @pl.when(has_prev)
    def _():
        to_prev.wait_send()


def per_device(
    columns,
    activations,
    dilated_tap_weight,
    conv_mix,
    w_query,
    w_keyval,
    contact_tiles,
    tile_codes,
    bin_valid,
):
    rows, channels = activations.shape
    hidden = conv_mix.shape[0]
    half_rows = rows // 2
    edge = 16
    count = lax.axis_size("seq")
    plane = 2 * columns
    far = -(-(HALF // rows) // plane)
    valid = jnp.where(bin_valid == 1, 0.0, masked_score).astype(jnp.float32)
    valid = valid.reshape(count, 1, rows)
    vmem = pl.BlockSpec(memory_space=pltpu.VMEM)
    smem = pl.BlockSpec(memory_space=pltpu.SMEM)
    hbm = pl.BlockSpec(memory_space=pl.ANY)
    bf16, f32 = jnp.bfloat16, jnp.float32
    return pl.pallas_call(
        functools.partial(layer_kernel, columns, count),
        out_shape=jax.ShapeDtypeStruct((rows, HDIM), bf16),
        in_specs=[hbm, hbm, hbm, hbm, hbm, vmem, smem, vmem],
        out_specs=vmem,
        scratch_shapes=[
            pltpu.VMEM(activations.shape, bf16),
            pltpu.VMEM(dilated_tap_weight.shape, bf16),
            pltpu.VMEM(conv_mix.shape, bf16),
            pltpu.VMEM(w_query.shape, bf16),
            pltpu.VMEM(w_keyval.shape, bf16),
            pltpu.VMEM((2, edge, channels), bf16),
            pltpu.VMEM((rows + 2 * edge, channels), bf16),
            pltpu.VMEM((half_rows, hidden), bf16),
            pltpu.VMEM((half_rows, channels), f32),
            pltpu.VMEM((half_rows, channels), bf16),
            pltpu.VMEM(contact_tiles.shape, f32),
            pltpu.VMEM((rows, HDIM), bf16),
            pltpu.VMEM((rows, rows), f32),
            pltpu.VMEM((rows, rows), bf16),
            pltpu.VMEM((count, rows, 2 * HDIM), bf16),
            pltpu.VMEM((rows, 1), f32),
            pltpu.VMEM((rows, 1), f32),
            pltpu.VMEM((rows, HDIM), f32),
            pltpu.SemaphoreType.DMA((7,)),
            pltpu.SemaphoreType.DMA((2,)),
            pltpu.SemaphoreType.DMA((2,)),
            pltpu.SemaphoreType.DMA((4, (2 * far + 1) * columns, 2)),
            pltpu.SemaphoreType.DMA((count, 2)),
        ],
        compiler_params=pltpu.CompilerParams(
            collective_id=0, has_side_effects=True, vmem_limit_bytes=56 * 1024 * 1024
        ),
        cost_estimate=pl.CostEstimate(
            flops=2 * rows * channels * (4 * hidden + 3 * HDIM) + 4 * rows * HDIM * 2 * HALF,
            bytes_accessed=14 * 1024 * 1024,
            transcendentals=rows * 2 * HALF,
        ),
    )(
        activations,
        dilated_tap_weight,
        conv_mix,
        w_query,
        w_keyval,
        contact_tiles,
        tile_codes,
        valid,
    )


def columns_of(mesh):
    along = mesh.devices.reshape(-1, mesh.shape["seq"])[0]
    first = along[0]
    if not hasattr(first, "coords"):
        return 2 if mesh.shape["seq"] == 16 else 1
    return sum(d.coords[2] == first.coords[2] for d in along) // 2


def solution(mesh):
    in_specs = (P(("grp", "seq"), None), P(), P(), P(), P(), P(), P(("grp", "seq"), None), P("grp"))
    out_specs = P(("grp", "seq"), None)
    return jax.shard_map(
        functools.partial(per_device, columns_of(mesh)),
        mesh=mesh,
        in_specs=in_specs,
        out_specs=out_specs,
        check_vma=False,
    )
```

time: 79.4 us -> 56.4 us (0.71)
  the two profiles are of different devices: /device:TPU:18 before, /device:TPU:12 now
where the time goes in v2:
time: 56.4 us; the launch traced here: 56.2 us
  Pallas kernels  53.2 us (94%)
  local copies, waits for them, and re-layouts  1.57 us (3%)
  other arithmetic  1.38 us (2%)
    pallas_call x1, Pallas kernels, per_device(): pl.pallas_call(functools.partial(layer_kernel, columns, count), out_shape...  53.2 us
    unnamed x1, local copies, waits for them, and re-layouts  1.57 us
    select_n x1, other arithmetic, per_device(): valid = jnp.where(bin_valid == 1, 0.0, masked_score).astype(jnp.float32)  1.38 us

profile of v2, /device:TPU:12, one launch (start us, length us, event | category | flops | bytes accessed | tf_op | source)
XLA Modules:
  0.0 56.2 jit_solution(6197092705766061597)
XLA Ops:
  0.0 1.4 %compare_select_fusion = f32[8192]{0:T(1024)} fusion(s32[8192]{0:T(1024)} %param.15), kind=kLoop, calls=%fused_computation | loop fusion | flops 16384 | bytes 65536 | tf_op jit(solution)/shard_map/jit(_where)/select_n | solution.py:415
  1.4 53.2 %shard_map.82 = bf16[512,128]{1,0:T(8,128)(2,1)} custom-call(bf16[512,1536]{1,0:T(8,128)(2,1)} %act_hbm.1, bf16[3,1536,768]{2,1,0:T(8,128)(2,1)} %taps_hbm.1, bf16[768,1536]{1,0:T(8,128)(2,1)} %mix_hbm.1, bf16[1536,128]{1,0:T(8,128)(2,1)} %wq_hbm.1, bf16[1536,256]{1,0:T(8,128)(2,1)} %wkv_hbm.1, bf16[16,128,128]{2,1,0:T(8,128)(2,1)} %tiles_ref.1, ...), custom_call_target="tpu_custom_call" | custom-call | flops 7583301632 | bytes 14680064 | tf_op jit(solution)/shard_map/pallas_call | solution.py:421
  54.6 1.6 %copy.10 = bf16[512,128]{1,0:T(8,128)(2,1)} copy(bf16[512,128]{1,0:T(8,128)(2,1)} %shard_map.82) | data formatting | bytes 262144

commit v3 on v2

--- a/solution.py
+++ b/solution.py
@@ -36,24 +36,52 @@
     def index(self, z, y, core):
         return z * self.plane + y * 2 + core
 
+    def order(self):
+        blocks = [(0, 0)]
+        late = [(0, 1)]
+        for d in range(1, self.far + 1):
+            if d == 1 and self.columns == 2:
+                blocks += late
+                late = []
+            blocks += [(-d, 0), (d, 0)]
+            if d > 1 and self.columns == 2:
+                blocks += late
+            late = [(-d, 1), (d, 1)]
+        if self.columns == 2:
+            blocks += late
+        return blocks
+
+    def hand_order(self):
+        blocks = self.order()
+        first = 3 if self.columns == 2 else 2
+        steps = [(1, k, 0) for k in range(1, first + 1)]
+        steps += [(2, k, 1) for k in range(1, first + 1)]
+        k, turn = first + 1, 4
+        while k < len(blocks):
+            steps += [(turn, k, 0), (turn, k + 1, 0)]
+            turn += 2
+            steps += [(turn, k, 1), (turn, k + 1, 1)]
+            k += 2
+        assert all(turn <= 2 * k for turn, k, _half in steps)
+        return steps
+
     def step(self, k):
-        kk = jnp.maximum(k - self.columns, 0)
-        rem = kk % (2 * self.columns)
-        late = k >= self.columns
-        dz = jnp.where(late, (kk // (2 * self.columns) + 1) * (2 * (rem % 2) - 1), 0)
-        flip = jnp.where(late, rem // 2, k)
+        dz = flip = jnp.int32(0)
+        for i, (d, f) in enumerate(self.order()):
+            dz = jnp.where(k == i, d, dz)
+            flip = jnp.where(k == i, f, flip)
         return dz, flip
 
     def needs(self, source, target):
         return jnp.abs(source - target) <= self.reach
 
 
-def block_moves(place, kvbuf, send_sem, recv_sem, dz, flip, half, rows):
+def block_moves(place, kvbuf, send_sem, recv_sem, dz, flip, half, part):
     z, y, core = place.z, place.y, place.core
     source_z = z + dz
     source = place.index(source_z, (y + flip) % 2 if place.columns == 2 else y, core)
     held = (source_z >= 0) & (source_z < place.planes) & place.needs(source, place.me)
-    piece = kvbuf.at[source, pl.ds(half * rows, rows)]
+    piece = kvbuf.at[source, pl.ds(half * part, part)]
     slot = (dz + place.far) * place.columns + flip
     edge = (source_z == 0) | (source_z == place.planes - 1)
     away = jnp.abs(dz)
@@ -88,7 +116,16 @@
 
 
 def gelu(v):
-    return 0.5 * v * (1.0 + lax.erf(v * math.sqrt(0.5)))
+    size = jnp.abs(v)
+    low = 1.0 + (0.3275911 * math.sqrt(0.5)) * size
+    t = pl.reciprocal(low, approx=True)
+    t = t * (2.0 - low * t)
+    poly = 0.5 * 1.061405429 * t - 0.5 * 1.453152027
+    poly = poly * t + 0.5 * 1.421413741
+    poly = poly * t - 0.5 * 0.284496736
+    poly = (poly * t + 0.5 * 0.254829592) * t
+    tail = poly * jnp.exp2((-0.5 * LOG2E) * (size * size))
+    return jnp.maximum(v, 0.0) - size * tail
 
 
 def layer_kernel(
@@ -99,9 +136,9 @@
     mix_hbm,
     wq_hbm,
     wkv_hbm,
+    mask_hbm,
     tiles_ref,
     codes_ref,
-    valid_ref,
     out_ref,
     act,
     taps,
@@ -115,11 +152,11 @@
     normed,
     table,
     queries,
+    mask,
     scores_buf,
     probs_buf,
     kvbuf,
     peak,
-    total,
     weighted,
     load_sem,
     halo_send,
@@ -145,6 +182,7 @@
         pltpu.make_async_copy(mix_hbm, mix, load_sem.at[4]),
         pltpu.make_async_copy(wq_hbm, wq, load_sem.at[5]),
         pltpu.make_async_copy(wkv_hbm, wkv, load_sem.at[6]),
+        pltpu.make_async_copy(mask_hbm, mask, load_sem.at[7]),
     ]
     for load in loads:
         load.start()
@@ -194,19 +232,20 @@
     def _():
         to_prev.start()
 
-    table[...] = tiles_ref[...].astype(jnp.float32) * LOG2E
+    for code in range(tiles_ref.shape[0]):
+        table[code] = tiles_ref[code].astype(jnp.float32).T * LOG2E
     peak[...] = jnp.full(peak.shape, masked_score, jnp.float32)
-    total[...] = jnp.zeros(total.shape, jnp.float32)
+    spare = lax.broadcasted_iota(jnp.int32, (HDIM, rows), 0) == 0
+    queries[HDIM:] = jnp.where(spare, 1.0, 0.0).astype(jnp.bfloat16)
     weighted[...] = jnp.zeros(weighted.shape, jnp.float32)
 
     def lift(strip, carry):
-        at = pl.multiple_of(strip * edge, edge)
-        lifted[pl.ds(at + edge, edge)] = gelu(act[pl.ds(at, edge)].astype(jnp.float32)).astype(
-            jnp.bfloat16
-        )
+        at = pl.multiple_of(strip * 2 * edge, 2 * edge)
+        raised = gelu(act[pl.ds(at, 2 * edge)].astype(jnp.float32))
+        lifted[pl.ds(at + edge, 2 * edge)] = raised.astype(jnp.bfloat16)
         return carry
 
-    lax.fori_loop(0, rows // edge, lift, 0)
+    lax.fori_loop(0, rows // (2 * edge), lift, 0)
 
     for side, there, copy in ((0, has_prev, to_next), (1, has_next, to_prev)):
         at = side * (rows + edge)
@@ -222,7 +261,7 @@
 
     def moves_of(k, half):
         dz, flip = place.step(k)
-        return block_moves(place, kvbuf, send_sem, recv_sem, dz, flip, half, half_rows)
+        return block_moves(place, kvbuf, send_sem, recv_sem, dz, flip, half, tiles // 2)
 
     def hand_on(held, moves):
         for go, copy in moves:
@@ -272,57 +311,65 @@
         for n in range(0, channels, wide):
             normed[:, n : n + wide] = (mixed[:, n : n + wide] * factor).astype(jnp.bfloat16)
         keyval = jnp.dot(normed[...], wkv[...], preferred_element_type=jnp.float32)
-        kvbuf[me, pl.ds(at, half_rows)] = keyval.astype(jnp.bfloat16)
+        keys = keyval[:, :HDIM].astype(jnp.bfloat16)
+        values = keyval[:, HDIM:].T.astype(jnp.bfloat16)
+        for j in range(tiles // 2):
+            here = slice(j * tile, (j + 1) * tile)
+            kvbuf[me, half * (tiles // 2) + j, :tile] = keys[here]
+            kvbuf[me, half * (tiles // 2) + j, tile:] = values[:, here]
         _source, held, moves = moves_of(0, half)
         hand_on(held, moves)
         query = jnp.dot(normed[...], wq[...], preferred_element_type=jnp.float32)
-        queries[pl.ds(at, half_rows)] = (query * (LOG2E / math.sqrt(HDIM))).astype(jnp.bfloat16)
+        query = (query * (LOG2E / math.sqrt(HDIM))).T.astype(jnp.bfloat16)
+
+        @pl.when(half == 0)
+        def _():
+            queries[:HDIM, :half_rows] = query
+
+        @pl.when(half == 1)
+        def _():
+            queries[:HDIM, half_rows:] = query
+
         return carry
 
     lax.fori_loop(0, 2, front, 0)
-
-    strip_rows = 32
 
     def absorb(source, special):
         delta = source - me
-        scores_buf[...] = lax.dot_general(
-            queries[...],
-            kvbuf[source, :, :HDIM],
-            (((1,), (1,)), ((), ())),
-            preferred_element_type=jnp.float32,
-        )
+        keys = jnp.concatenate([kvbuf[source, j, :tile] for j in range(tiles)], axis=0)
+        values = jnp.concatenate([kvbuf[source, j, tile:] for j in range(tiles)], axis=1)
+        values = jnp.concatenate([values, jnp.ones((16, rows), jnp.bfloat16)], axis=0)
+        if special:
+            scores_buf[...] = jnp.dot(
+                keys, queries[:HDIM], preferred_element_type=jnp.float32
+            )
+        else:
+            keys = jnp.concatenate([keys, mask[source]], axis=1)
+            scores_buf[...] = jnp.dot(keys, queries[...], preferred_element_type=jnp.float32)
         shrinks = []
         for i in range(tiles):
-            codes = []
+            across = slice(i * tile, (i + 1) * tile)
+            column = []
             for j in range(tiles):
                 offset = jnp.clip(delta * tiles + (j - i) + offsets // 2, 0, offsets - 1)
-                codes.append(codes_ref[i, offset])
-            for r in range(0, tile, strip_rows):
-                at = i * tile + r
-                bias = jnp.concatenate(
-                    [table[code, r : r + strip_rows] for code in codes], axis=1
-                )
-                scores = scores_buf[at : at + strip_rows] + bias
+                scores = scores_buf[j * tile : (j + 1) * tile, across] + table[codes_ref[i, offset]]
                 if special:
-                    row = lax.broadcasted_iota(jnp.int32, (strip_rows, rows), 0) + at
-                    col = lax.broadcasted_iota(jnp.int32, (strip_rows, rows), 1)
-                    apart = delta * rows + col - row
-                    kept = (jnp.abs(apart) <= HALF) & (valid_ref[source] >= 0.0)
-                    scores = jnp.where((apart == 0) | kept, scores, masked_score)
-                else:
-                    scores = scores + valid_ref[source]
-                old = peak[at : at + strip_rows]
-                new = jnp.maximum(old, jnp.max(scores, axis=1, keepdims=True))
-                probs = jnp.exp2(scores - new)
-                shrink = jnp.exp2(old - new)
-                peak[at : at + strip_rows] = new
-                total[at : at + strip_rows] = total[at : at + strip_rows] * shrink + jnp.sum(
-                    probs, axis=1, keepdims=True
-                )
-                weighted[at : at + strip_rows] = weighted[at : at + strip_rows] * shrink
-                probs_buf[at : at + strip_rows] = probs.astype(jnp.bfloat16)
-        weighted[...] += jnp.dot(
-            probs_buf[...], kvbuf[source, :, HDIM:], preferred_element_type=jnp.float32
+                    key_row = lax.broadcasted_iota(jnp.int32, (tile, tile), 0) + j * tile
+                    query_row = lax.broadcasted_iota(jnp.int32, (tile, tile), 1) + i * tile
+                    apart = delta * rows + key_row - query_row
+                    usable = mask[source, j * tile : (j + 1) * tile].astype(jnp.float32) >= 0.0
+                    kept = (apart == 0) | ((jnp.abs(apart) <= HALF) & usable)
+                    scores = jnp.where(kept, scores, masked_score)
+                column.append(scores)
+            column = jnp.concatenate(column, axis=0)
+            old = peak[:, across]
+            new = jnp.maximum(old, jnp.max(column, axis=0, keepdims=True))
+            probs_buf[:, across] = jnp.exp2(column - new).astype(jnp.bfloat16)
+            peak[:, across] = new
+            shrinks.append(jnp.exp2(old - new))
+        shrink = jnp.concatenate(shrinks, axis=1)
+        weighted[...] = weighted[...] * shrink + jnp.dot(
+            values, probs_buf[...], preferred_element_type=jnp.float32
         )
 
     def absorb_block(source):
@@ -338,39 +385,52 @@
             absorb(source, False)
 
     def arrived(source, half):
-        piece = kvbuf.at[source, pl.ds(half * half_rows, half_rows)]
+        piece = kvbuf.at[source, pl.ds(half * (tiles // 2), tiles // 2)]
         pltpu.make_async_copy(piece, piece, recv_sem.at[source, half]).wait()
 
-    def turn_of(k, carry):
-        for half in range(2):
-            source, held, moves = moves_of(k, half)
-            held = held & (k < place.steps)
-
-            @pl.when(held & (k > 0))
+    hand_steps = place.hand_order()
+    turns = 2 * place.steps
+
+    def hand_one(c, carry):
+        k = half = jnp.int32(0)
+        for i, (_turn, block, part) in enumerate(hand_steps):
+            k = jnp.where(c == i, block, k)
+            half = jnp.where(c == i, part, half)
+        source, held, moves = moves_of(k, half)
+
+        @pl.when(held)
+        def _():
+            arrived(source, half)
+
+        hand_on(held, moves)
+        return carry
+
+    def turn_of(u, done):
+        until = jnp.int32(0)
+        for turn, _block, _part in hand_steps:
+            until = until + jnp.where(turn <= u, 1, 0)
+        lax.fori_loop(done, until, hand_one, 0)
+        dz, flip = place.step(u // 2)
+        away = u % 2
+        source_z = z + dz
+        column = (y + flip) % 2 if columns == 2 else y
+        source = place.index(source_z, column, (core + away) % 2)
+        take = (source_z >= 0) & (source_z < place.planes) & place.needs(source, me)
+
+        @pl.when(take)
+        def _():
+            @pl.when(away == 1)
             def _():
-                arrived(source, half)
-
-            hand_on(held & (k > 0), moves)
-
-        dz, flip = place.step(jnp.maximum(k - 1, 0))
-        other_z = z + dz
-        other = place.index(other_z, (y + flip) % 2 if columns == 2 else y, 1 - core)
-        take = (k > 0) & (other_z >= 0) & (other_z < place.planes) & place.needs(other, me)
-
-        @pl.when(held)
-        def _():
+                arrived(source, 0)
+                arrived(source, 1)
+
             absorb_block(source)
 
-        @pl.when(take)
-        def _():
-            arrived(other, 0)
-            arrived(other, 1)
-            absorb_block(other)
-
-        return carry
-
-    lax.fori_loop(0, place.steps + 1, turn_of, 0)
-    out_ref[...] = (weighted[...] / total[...]).astype(out_ref.dtype)
+        return until
+
+    lax.fori_loop(0, turns, turn_of, jnp.int32(0))
+    result = weighted[:HDIM] / weighted[HDIM : HDIM + 1]
+    out_ref[...] = result.T.astype(out_ref.dtype)
 
     def drain(k, carry):
         for half in range(2):
@@ -409,11 +469,12 @@
     hidden = conv_mix.shape[0]
     half_rows = rows // 2
     edge = 16
+    tile = contact_tiles.shape[1]
     count = lax.axis_size("seq")
     plane = 2 * columns
     far = -(-(HALF // rows) // plane)
-    valid = jnp.where(bin_valid == 1, 0.0, masked_score).astype(jnp.float32)
-    valid = valid.reshape(count, 1, rows)
+    mask = jnp.where(bin_valid == 1, 0.0, masked_score).astype(jnp.bfloat16)
+    mask = jnp.broadcast_to(mask.reshape(count, rows, 1), (count, rows, HDIM))
     vmem = pl.BlockSpec(memory_space=pltpu.VMEM)
     smem = pl.BlockSpec(memory_space=pltpu.SMEM)
     hbm = pl.BlockSpec(memory_space=pl.ANY)
@@ -421,7 +482,7 @@
     return pl.pallas_call(
         functools.partial(layer_kernel, columns, count),
         out_shape=jax.ShapeDtypeStruct((rows, HDIM), bf16),
-        in_specs=[hbm, hbm, hbm, hbm, hbm, vmem, smem, vmem],
+        in_specs=[hbm, hbm, hbm, hbm, hbm, hbm, vmem, smem],
         out_specs=vmem,
         scratch_shapes=[
             pltpu.VMEM(activations.shape, bf16),
@@ -435,14 +496,14 @@
             pltpu.VMEM((half_rows, channels), f32),
             pltpu.VMEM((half_rows, channels), bf16),
             pltpu.VMEM(contact_tiles.shape, f32),
-            pltpu.VMEM((rows, HDIM), bf16),
+            pltpu.VMEM((2 * HDIM, rows), bf16),
+            pltpu.VMEM(mask.shape, bf16),
             pltpu.VMEM((rows, rows), f32),
             pltpu.VMEM((rows, rows), bf16),
-            pltpu.VMEM((count, rows, 2 * HDIM), bf16),
-            pltpu.VMEM((rows, 1), f32),
-            pltpu.VMEM((rows, 1), f32),
-            pltpu.VMEM((rows, HDIM), f32),
-            pltpu.SemaphoreType.DMA((7,)),
+            pltpu.VMEM((count, rows // tile, 2 * tile, HDIM), bf16),
+            pltpu.VMEM((1, rows), f32),
+            pltpu.VMEM((HDIM + 16, rows), f32),
+            pltpu.SemaphoreType.DMA((8,)),
             pltpu.SemaphoreType.DMA((2,)),
             pltpu.SemaphoreType.DMA((2,)),
             pltpu.SemaphoreType.DMA((4, (2 * far + 1) * columns, 2)),
@@ -462,9 +523,9 @@
         conv_mix,
         w_query,
         w_keyval,
+        mask,
         contact_tiles,
         tile_codes,
-        valid,
     )
 
 

time: 56.4 us -> 44.9 us (0.80)
  Pallas kernels: 53.2 us -> 40 us
  local copies, waits for them, and re-layouts: 1.57 us -> 3.87 us
  other arithmetic: 1.38 us -> 0.76 us
    pallas_call x1, Pallas kernels: 53.2 us -> 40 us  [per_device(): pl.pallas_call(functools.partial(layer_kernel, columns, count), out_shape...]
    broadcast_in_dim x0 -> x2, local copies, waits for them, and re-layouts: none -> 2.3 us  [per_device(): mask = jnp.broadcast_to(mask.reshape(count, rows, 1), (count, rows, HDIM))]
    select_n x1 -> x0, other arithmetic: 1.38 us -> none  [per_device(): valid = jnp.where(bin_valid == 1, 0.0, masked_score).astype(jnp.float32)]
    convert_element_type x0 -> x1, other arithmetic: none -> 0.76 us  [per_device(): mask = jnp.where(bin_valid == 1, 0.0, masked_score).astype(jnp.bfloat16)]
where the time goes in v3:
time: 44.9 us; the launch traced here: 44.6 us
  Pallas kernels  40 us (89%)
  local copies, waits for them, and re-layouts  3.87 us (9%)
  other arithmetic  0.76 us (2%)
    pallas_call x1, Pallas kernels, per_device(): pl.pallas_call(functools.partial(layer_kernel, columns, count), out_shape...  40 us
    broadcast_in_dim x2, local copies, waits for them, and re-layouts, per_device(): mask = jnp.broadcast_to(mask.reshape(count, rows, 1), (count, rows, HDIM))  2.3 us
    unnamed x1, local copies, waits for them, and re-layouts  1.57 us

profile of v3, /device:TPU:12, one launch (start us, length us, event | category | flops | bytes accessed | tf_op | source)
XLA Modules:
  0.0 44.6 jit_solution(15732386801114202573)
XLA Ops:
  0.0 0.8 %select_convert_fusion = bf16[8192]{0:T(1024)(128)(2,1)S(1)} fusion(s32[8192]{0:T(1024)} %param.15), kind=kLoop, calls=%fused_computation | loop fusion | flops 24576 | bytes 49152 | tf_op jit(solution)/shard_map/convert_element_type | solution.py:476
  0.8 2.3 %broadcast_in_dim.18.mask_hbm = bf16[16,512,128]{2,1,0:T(8,128)(2,1)} broadcast(bf16[16,512]{1,0:T(8,128)(2,1)S(1)} %broadcast_in_dim.17), dimensions={0,1} | broadcast | bytes 2113536 | tf_op jit(solution)/shard_map/broadcast_in_dim | solution.py:477
  3.1 40.0 %shard_map.82 = bf16[512,128]{1,0:T(8,128)(2,1)} custom-call(bf16[512,1536]{1,0:T(8,128)(2,1)} %act_hbm.1, bf16[3,1536,768]{2,1,0:T(8,128)(2,1)} %taps_hbm.1, bf16[768,1536]{1,0:T(8,128)(2,1)} %mix_hbm.1, bf16[1536,128]{1,0:T(8,128)(2,1)} %wq_hbm.1, bf16[1536,256]{1,0:T(8,128)(2,1)} %wkv_hbm.1, bf16[16,512,128]{2,1,0:T(8,128)(2,1)} %broadcast_in_dim.18.mask_hbm, ...), custom_call_target="tpu_custom_call" | custom-call | flops 7583301632 | bytes 14680064 | tf_op jit(solution)/shard_map/pallas_call | solution.py:482
  43.1 1.6 %copy.10 = bf16[512,128]{1,0:T(8,128)(2,1)} copy(bf16[512,128]{1,0:T(8,128)(2,1)} %shard_map.82) | data formatting | bytes 262144
  (1 shorter events, 0.0 us)

commit v4 on v3

--- a/solution.py
+++ b/solution.py
@@ -53,17 +53,17 @@
 
     def hand_order(self):
         blocks = self.order()
-        first = 3 if self.columns == 2 else 2
-        steps = [(1, k, 0) for k in range(1, first + 1)]
+        first = self.near()
+        steps = [(0, k, 0) for k in range(1, first + 1)]
         steps += [(2, k, 1) for k in range(1, first + 1)]
-        k, turn = first + 1, 4
-        while k < len(blocks):
-            steps += [(turn, k, 0), (turn, k + 1, 0)]
-            turn += 2
-            steps += [(turn, k, 1), (turn, k + 1, 1)]
-            k += 2
-        assert all(turn <= 2 * k for turn, k, _half in steps)
+        for k in range(first + 1, len(blocks), 2):
+            early = 2 if self.columns == 2 and k == first + 1 else 0
+            steps += [(2 * k - 2 - early, k, 0), (2 * k - 2 - early, k + 1, 0)]
+            steps += [(2 * k - early, k, 1), (2 * k - early, k + 1, 1)]
         return steps
+
+    def near(self):
+        return 3 if self.columns == 2 else 2
 
     def step(self, k):
         dz = flip = jnp.int32(0)
@@ -136,9 +136,9 @@
     mix_hbm,
     wq_hbm,
     wkv_hbm,
-    mask_hbm,
     tiles_ref,
     codes_ref,
+    valid_ref,
     out_ref,
     act,
     taps,
@@ -152,7 +152,6 @@
     normed,
     table,
     queries,
-    mask,
     scores_buf,
     probs_buf,
     kvbuf,
@@ -171,18 +170,25 @@
     tiles = rows // tile
     offsets = codes_ref.shape[1]
     edge = halo.shape[1]
+    early_rows = half_rows + 2 * edge
     place = Place(count, columns, HALF // rows)
     me, z, y, core = place.me, place.z, place.y, place.core
 
     loads = [
-        pltpu.make_async_copy(act_hbm, act, load_sem.at[0]),
+        pltpu.make_async_copy(
+            act_hbm.at[pl.ds(0, early_rows)], act.at[pl.ds(0, early_rows)], load_sem.at[0]
+        ),
+        pltpu.make_async_copy(
+            act_hbm.at[pl.ds(early_rows, rows - early_rows)],
+            act.at[pl.ds(early_rows, rows - early_rows)],
+            load_sem.at[7],
+        ),
         pltpu.make_async_copy(taps_hbm.at[0], taps.at[0], load_sem.at[1]),
         pltpu.make_async_copy(taps_hbm.at[1], taps.at[1], load_sem.at[2]),
         pltpu.make_async_copy(taps_hbm.at[2], taps.at[2], load_sem.at[3]),
         pltpu.make_async_copy(mix_hbm, mix, load_sem.at[4]),
         pltpu.make_async_copy(wq_hbm, wq, load_sem.at[5]),
         pltpu.make_async_copy(wkv_hbm, wkv, load_sem.at[6]),
-        pltpu.make_async_copy(mask_hbm, mask, load_sem.at[7]),
     ]
     for load in loads:
         load.start()
@@ -203,6 +209,7 @@
             pl.semaphore_signal(barrier, inc=1, device_id={"seq": target}, device_id_type=MESH)
 
     loads[0].wait()
+    loads[1].wait()
     pl.semaphore_wait(barrier, sum(ok.astype(jnp.int32) for ok, _target in greeted))
 
     has_next = me + 1 < count
@@ -232,22 +239,25 @@
     def _():
         to_prev.start()
 
-    for code in range(tiles_ref.shape[0]):
-        table[code] = tiles_ref[code].astype(jnp.float32).T * LOG2E
     peak[...] = jnp.full(peak.shape, masked_score, jnp.float32)
     spare = lax.broadcasted_iota(jnp.int32, (HDIM, rows), 0) == 0
     queries[HDIM:] = jnp.where(spare, 1.0, 0.0).astype(jnp.bfloat16)
     weighted[...] = jnp.zeros(weighted.shape, jnp.float32)
 
-    def lift(strip, carry):
-        at = pl.multiple_of(strip * 2 * edge, 2 * edge)
-        raised = gelu(act[pl.ds(at, 2 * edge)].astype(jnp.float32))
-        lifted[pl.ds(at + edge, 2 * edge)] = raised.astype(jnp.bfloat16)
+    def lift(at, count):
+        raised = gelu(act[pl.ds(at, count)].astype(jnp.float32))
+        lifted[pl.ds(at + edge, count)] = raised.astype(jnp.bfloat16)
+
+    def lift_strip(strip, carry):
+        lift(pl.multiple_of(strip * 2 * edge, 2 * edge), 2 * edge)
         return carry
 
-    lax.fori_loop(0, rows // (2 * edge), lift, 0)
-
-    for side, there, copy in ((0, has_prev, to_next), (1, has_next, to_prev)):
+    def turn_tile(code):
+        table[code] = tiles_ref[code].astype(jnp.float32).T * LOG2E
+
+    lax.fori_loop(0, early_rows // (2 * edge), lift_strip, 0)
+
+    def lift_halo(side, there, copy):
         at = side * (rows + edge)
 
         @pl.when(there)
@@ -258,6 +268,8 @@
         @pl.when(jnp.logical_not(there))
         def _():
             lifted[at : at + edge] = jnp.zeros((edge, channels), jnp.bfloat16)
+
+    lift_halo(0, has_prev, to_next)
 
     def moves_of(k, half):
         dz, flip = place.step(k)
@@ -270,37 +282,63 @@
             def _():
                 copy.start()
 
-    for load in loads[1:]:
+    def arrived(source, half):
+        piece = kvbuf.at[source, pl.ds(half * (tiles // 2), tiles // 2)]
+        pltpu.make_async_copy(piece, piece, recv_sem.at[source, half]).wait()
+
+    hand_steps = place.hand_order()
+
+    def hand_one(c, carry):
+        k = half = jnp.int32(0)
+        for i, (_turn, block, part) in enumerate(hand_steps):
+            k = jnp.where(c == i, block, k)
+            half = jnp.where(c == i, part, half)
+        source, held, moves = moves_of(k, half)
+
+        @pl.when(held)
+        def _():
+            arrived(source, half)
+
+        hand_on(held, moves)
+        return carry
+
+    for load in loads[2:5]:
         load.wait()
 
     wide = 256
     shift = CONV_DILATION
-
-    def front(half, carry):
-        at = pl.multiple_of(half * half_rows, half_rows)
-        tall = half_rows + edge
-        for n in range(0, hidden, wide):
+    tall = half_rows + edge
+
+    def convolve(half, beside):
+        at = half * half_rows
+        parts = hidden // wide
+        for p in range(parts):
+            cols = slice(p * wide, (p + 1) * wide)
             low = jnp.dot(
-                lifted[pl.ds(at, tall)],
-                taps[0, :, n : n + wide],
-                preferred_element_type=jnp.float32,
+                lifted[at : at + tall], taps[0, :, cols], preferred_element_type=jnp.float32
             )
             mid = jnp.dot(
-                lifted[pl.ds(at + edge, half_rows)],
-                taps[1, :, n : n + wide],
+                lifted[at + edge : at + edge + half_rows],
+                taps[1, :, cols],
                 preferred_element_type=jnp.float32,
             )
             high = jnp.dot(
-                lifted[pl.ds(at + edge, tall)],
-                taps[2, :, n : n + wide],
+                lifted[at + edge : at + edge + tall],
+                taps[2, :, cols],
                 preferred_element_type=jnp.float32,
             )
+            for task in beside[p::parts]:
+                task()
             conv = low[edge - shift : edge - shift + half_rows] + mid
             conv = conv + high[shift : shift + half_rows]
-            squeezed[:, n : n + wide] = gelu(conv).astype(jnp.bfloat16)
+            squeezed[:, cols] = gelu(conv).astype(jnp.bfloat16)
+
+    def project(half):
+        at = half * half_rows
+        here = slice(at, at + half_rows)
         square = jnp.zeros((half_rows, 128), jnp.float32)
         for n in range(0, channels, wide):
-            part = act[pl.ds(at, half_rows), n : n + wide].astype(jnp.float32) + jnp.dot(
+            part = act[here, n : n + wide].astype(jnp.float32) + jnp.dot(
                 squeezed[...], mix[:, n : n + wide], preferred_element_type=jnp.float32
             )
             mixed[:, n : n + wide] = part
@@ -314,37 +352,48 @@
         keys = keyval[:, :HDIM].astype(jnp.bfloat16)
         values = keyval[:, HDIM:].T.astype(jnp.bfloat16)
         for j in range(tiles // 2):
-            here = slice(j * tile, (j + 1) * tile)
-            kvbuf[me, half * (tiles // 2) + j, :tile] = keys[here]
-            kvbuf[me, half * (tiles // 2) + j, tile:] = values[:, here]
+            cut = slice(j * tile, (j + 1) * tile)
+            kvbuf[me, half * (tiles // 2) + j, :tile] = keys[cut]
+            kvbuf[me, half * (tiles // 2) + j, tile:] = values[:, cut]
         _source, held, moves = moves_of(0, half)
         hand_on(held, moves)
         query = jnp.dot(normed[...], wq[...], preferred_element_type=jnp.float32)
         query = (query * (LOG2E / math.sqrt(HDIM))).T.astype(jnp.bfloat16)
-
-        @pl.when(half == 0)
-        def _():
-            queries[:HDIM, :half_rows] = query
-
-        @pl.when(half == 1)
-        def _():
-            queries[:HDIM, half_rows:] = query
-
-        return carry
-
-    lax.fori_loop(0, 2, front, 0)
+        queries[:HDIM, here] = query
+
+    beside = [
+        functools.partial(lift, at, edge) for at in range(early_rows, rows, edge)
+    ] + [functools.partial(turn_tile, code) for code in range(tiles_ref.shape[0])]
+    convolve(0, beside)
+    for load in loads[5:]:
+        load.wait()
+    project(0)
+    lift_halo(1, has_next, to_prev)
+    convolve(1, [])
+    lax.fori_loop(0, place.near(), hand_one, 0)
+    project(1)
 
     def absorb(source, special):
         delta = source - me
         keys = jnp.concatenate([kvbuf[source, j, :tile] for j in range(tiles)], axis=0)
         values = jnp.concatenate([kvbuf[source, j, tile:] for j in range(tiles)], axis=1)
         values = jnp.concatenate([values, jnp.ones((16, rows), jnp.bfloat16)], axis=0)
+        lanes = tile
+        line = [valid_ref[pl.ds(source * tiles + j, 1)] for j in range(tiles)]
+        line = jnp.where(jnp.concatenate(line, axis=1) == 1, 0.0, masked_score)
+        line = jnp.broadcast_to(line, (16, rows)).astype(jnp.bfloat16)
+        mask = lax.dot_general(
+            line,
+            jnp.ones((16, lanes), jnp.bfloat16),
+            (((0,), (0,)), ((), ())),
+            preferred_element_type=jnp.float32,
+        )
         if special:
             scores_buf[...] = jnp.dot(
                 keys, queries[:HDIM], preferred_element_type=jnp.float32
             )
         else:
-            keys = jnp.concatenate([keys, mask[source]], axis=1)
+            keys = jnp.concatenate([keys, mask.astype(jnp.bfloat16)], axis=1)
             scores_buf[...] = jnp.dot(keys, queries[...], preferred_element_type=jnp.float32)
         shrinks = []
         for i in range(tiles):
@@ -357,7 +406,7 @@
                     key_row = lax.broadcasted_iota(jnp.int32, (tile, tile), 0) + j * tile
                     query_row = lax.broadcasted_iota(jnp.int32, (tile, tile), 1) + i * tile
                     apart = delta * rows + key_row - query_row
-                    usable = mask[source, j * tile : (j + 1) * tile].astype(jnp.float32) >= 0.0
+                    usable = mask[j * tile : (j + 1) * tile] >= 0.0
                     kept = (apart == 0) | ((jnp.abs(apart) <= HALF) & usable)
                     scores = jnp.where(kept, scores, masked_score)
                 column.append(scores)
@@ -384,11 +433,6 @@
         def _():
             absorb(source, False)
 
-    def arrived(source, half):
-        piece = kvbuf.at[source, pl.ds(half * (tiles // 2), tiles // 2)]
-        pltpu.make_async_copy(piece, piece, recv_sem.at[source, half]).wait()
-
-    hand_steps = place.hand_order()
     turns = 2 * place.steps
 
     def hand_one(c, carry):
@@ -428,7 +472,7 @@
 
         return until
 
-    lax.fori_loop(0, turns, turn_of, jnp.int32(0))
+    lax.fori_loop(0, turns, turn_of, jnp.int32(place.near()))
     result = weighted[:HDIM] / weighted[HDIM : HDIM + 1]
     out_ref[...] = result.T.astype(out_ref.dtype)
 
@@ -473,8 +517,7 @@
     count = lax.axis_size("seq")
     plane = 2 * columns
     far = -(-(HALF // rows) // plane)
-    mask = jnp.where(bin_valid == 1, 0.0, masked_score).astype(jnp.bfloat16)
-    mask = jnp.broadcast_to(mask.reshape(count, rows, 1), (count, rows, HDIM))
+    valid = bin_valid.reshape(count * rows // tile, tile)
     vmem = pl.BlockSpec(memory_space=pltpu.VMEM)
     smem = pl.BlockSpec(memory_space=pltpu.SMEM)
     hbm = pl.BlockSpec(memory_space=pl.ANY)
@@ -482,7 +525,7 @@
     return pl.pallas_call(
         functools.partial(layer_kernel, columns, count),
         out_shape=jax.ShapeDtypeStruct((rows, HDIM), bf16),
-        in_specs=[hbm, hbm, hbm, hbm, hbm, hbm, vmem, smem],
+        in_specs=[hbm, hbm, hbm, hbm, hbm, vmem, smem, vmem],
         out_specs=vmem,
         scratch_shapes=[
             pltpu.VMEM(activations.shape, bf16),
@@ -497,7 +540,6 @@
             pltpu.VMEM((half_rows, channels), bf16),
             pltpu.VMEM(contact_tiles.shape, f32),
             pltpu.VMEM((2 * HDIM, rows), bf16),
-            pltpu.VMEM(mask.shape, bf16),
             pltpu.VMEM((rows, rows), f32),
             pltpu.VMEM((rows, rows), bf16),
             pltpu.VMEM((count, rows // tile, 2 * tile, HDIM), bf16),
@@ -523,9 +565,9 @@
         conv_mix,
         w_query,
         w_keyval,
-        mask,
         contact_tiles,
         tile_codes,
+        valid,
     )
 
 

time: 44.9 us -> 42.2 us (0.940)
  the two profiles are of different devices: /device:TPU:12 before, /device:TPU:18 now
where the time goes in v4:
time: 42.2 us; the launch traced here: 41.7 us
  Pallas kernels  40.1 us (95%)
  local copies, waits for them, and re-layouts  1.57 us (4%)
    pallas_call x1, Pallas kernels, per_device(): pl.pallas_call(functools.partial(layer_kernel, columns, count), out_shape...  40.1 us
    unnamed x1, local copies, waits for them, and re-layouts  1.57 us

profile of v4, /device:TPU:18, one launch (start us, length us, event | category | flops | bytes accessed | tf_op | source)
XLA Modules:
  0.0 41.7 jit_solution(17161127295596843311)
XLA Ops:
  0.0 40.1 %shard_map.82 = bf16[512,128]{1,0:T(8,128)(2,1)} custom-call(bf16[512,1536]{1,0:T(8,128)(2,1)} %act_hbm.1, bf16[3,1536,768]{2,1,0:T(8,128)(2,1)} %taps_hbm.1, bf16[768,1536]{1,0:T(8,128)(2,1)} %mix_hbm.1, bf16[1536,128]{1,0:T(8,128)(2,1)} %wq_hbm.1, bf16[1536,256]{1,0:T(8,128)(2,1)} %wkv_hbm.1, bf16[16,128,128]{2,1,0:T(8,128)(2,1)} %tiles_ref.1, ...), custom_call_target="tpu_custom_call" | custom-call | flops 7583301632 | bytes 14680064 | tf_op jit(solution)/shard_map/pallas_call | solution.py:525
  40.1 1.6 %copy.10 = bf16[512,128]{1,0:T(8,128)(2,1)} copy(bf16[512,128]{1,0:T(8,128)(2,1)} %shard_map.82) | data formatting | bytes 262144

commit v5 on v4

--- a/solution.py
+++ b/solution.py
@@ -152,6 +152,7 @@
     normed,
     table,
     queries,
+    mask,
     scores_buf,
     probs_buf,
     kvbuf,
@@ -174,6 +175,8 @@
     place = Place(count, columns, HALF // rows)
     me, z, y, core = place.me, place.z, place.y, place.core
 
+    wide = 256
+    parts = hidden // wide
     loads = [
         pltpu.make_async_copy(
             act_hbm.at[pl.ds(0, early_rows)], act.at[pl.ds(0, early_rows)], load_sem.at[0]
@@ -181,14 +184,19 @@
         pltpu.make_async_copy(
             act_hbm.at[pl.ds(early_rows, rows - early_rows)],
             act.at[pl.ds(early_rows, rows - early_rows)],
-            load_sem.at[7],
+            load_sem.at[1],
         ),
-        pltpu.make_async_copy(taps_hbm.at[0], taps.at[0], load_sem.at[1]),
-        pltpu.make_async_copy(taps_hbm.at[1], taps.at[1], load_sem.at[2]),
-        pltpu.make_async_copy(taps_hbm.at[2], taps.at[2], load_sem.at[3]),
-        pltpu.make_async_copy(mix_hbm, mix, load_sem.at[4]),
-        pltpu.make_async_copy(wq_hbm, wq, load_sem.at[5]),
-        pltpu.make_async_copy(wkv_hbm, wkv, load_sem.at[6]),
+    ]
+    tap_loads = []
+    for p in range(parts):
+        cols = pl.ds(p * wide, wide)
+        tap_loads.append(
+            pltpu.make_async_copy(taps_hbm.at[:, :, cols], taps.at[:, :, cols], load_sem.at[5 + p])
+        )
+    late_loads = [
+        pltpu.make_async_copy(mix_hbm, mix, load_sem.at[2]),
+        pltpu.make_async_copy(wkv_hbm, wkv, load_sem.at[3]),
+        pltpu.make_async_copy(wq_hbm, wq, load_sem.at[4]),
     ]
     for load in loads:
         load.start()
@@ -209,6 +217,8 @@
             pl.semaphore_signal(barrier, inc=1, device_id={"seq": target}, device_id_type=MESH)
 
     loads[0].wait()
+    for load in tap_loads + late_loads:
+        load.start()
     loads[1].wait()
     pl.semaphore_wait(barrier, sum(ok.astype(jnp.int32) for ok, _target in greeted))
 
@@ -269,7 +279,30 @@
         def _():
             lifted[at : at + edge] = jnp.zeros((edge, channels), jnp.bfloat16)
 
+    for code in range(tiles_ref.shape[0]):
+        turn_tile(code)
+
+    def mask_of(d, carry):
+        source = me + d - place.reach
+
+        @pl.when((source >= 0) & (source < count))
+        def _():
+            line = [valid_ref[pl.ds(source * tiles + j, 1)] for j in range(tiles)]
+            line = jnp.where(jnp.concatenate(line, axis=1) == 1, 0.0, masked_score)
+            line = jnp.broadcast_to(line, (16, rows)).astype(jnp.bfloat16)
+            spread = lax.dot_general(
+                line,
+                jnp.ones((16, HDIM), jnp.bfloat16),
+                (((0,), (0,)), ((), ())),
+                preferred_element_type=jnp.float32,
+            )
+            mask[source] = spread.astype(jnp.bfloat16)
+
+        return carry
+
+    lax.fori_loop(0, 2 * place.reach + 1, mask_of, 0)
     lift_halo(0, has_prev, to_next)
+    lift_halo(1, has_next, to_prev)
 
     def moves_of(k, half):
         dz, flip = place.step(k)
@@ -302,18 +335,15 @@
         hand_on(held, moves)
         return carry
 
-    for load in loads[2:5]:
-        load.wait()
-
-    wide = 256
     shift = CONV_DILATION
     tall = half_rows + edge
 
     def convolve(half, beside):
         at = half * half_rows
-        parts = hidden // wide
         for p in range(parts):
             cols = slice(p * wide, (p + 1) * wide)
+            if half == 0:
+                tap_loads[p].wait()
             low = jnp.dot(
                 lifted[at : at + tall], taps[0, :, cols], preferred_element_type=jnp.float32
             )
@@ -361,14 +391,11 @@
         query = (query * (LOG2E / math.sqrt(HDIM))).T.astype(jnp.bfloat16)
         queries[:HDIM, here] = query
 
-    beside = [
-        functools.partial(lift, at, edge) for at in range(early_rows, rows, edge)
-    ] + [functools.partial(turn_tile, code) for code in range(tiles_ref.shape[0])]
+    beside = [functools.partial(lift, at, edge) for at in range(early_rows, rows, edge)]
     convolve(0, beside)
-    for load in loads[5:]:
+    for load in late_loads:
         load.wait()
     project(0)
-    lift_halo(1, has_next, to_prev)
     convolve(1, [])
     lax.fori_loop(0, place.near(), hand_one, 0)
     project(1)
@@ -378,48 +405,49 @@
         keys = jnp.concatenate([kvbuf[source, j, :tile] for j in range(tiles)], axis=0)
         values = jnp.concatenate([kvbuf[source, j, tile:] for j in range(tiles)], axis=1)
         values = jnp.concatenate([values, jnp.ones((16, rows), jnp.bfloat16)], axis=0)
-        lanes = tile
-        line = [valid_ref[pl.ds(source * tiles + j, 1)] for j in range(tiles)]
-        line = jnp.where(jnp.concatenate(line, axis=1) == 1, 0.0, masked_score)
-        line = jnp.broadcast_to(line, (16, rows)).astype(jnp.bfloat16)
-        mask = lax.dot_general(
-            line,
-            jnp.ones((16, lanes), jnp.bfloat16),
-            (((0,), (0,)), ((), ())),
-            preferred_element_type=jnp.float32,
-        )
         if special:
-            scores_buf[...] = jnp.dot(
-                keys, queries[:HDIM], preferred_element_type=jnp.float32
+            looked = queries.at[:HDIM]
+        else:
+            keys = jnp.concatenate([keys, mask[source]], axis=1)
+            looked = queries
+        spans = [slice(n, n + 2 * tile) for n in range(0, rows, 2 * tile)]
+        for span in spans:
+            scores_buf[:, span] = jnp.dot(
+                keys, looked[:, span], preferred_element_type=jnp.float32
             )
-        else:
-            keys = jnp.concatenate([keys, mask.astype(jnp.bfloat16)], axis=1)
-            scores_buf[...] = jnp.dot(keys, queries[...], preferred_element_type=jnp.float32)
-        shrinks = []
-        for i in range(tiles):
-            across = slice(i * tile, (i + 1) * tile)
-            column = []
-            for j in range(tiles):
-                offset = jnp.clip(delta * tiles + (j - i) + offsets // 2, 0, offsets - 1)
-                scores = scores_buf[j * tile : (j + 1) * tile, across] + table[codes_ref[i, offset]]
-                if special:
-                    key_row = lax.broadcasted_iota(jnp.int32, (tile, tile), 0) + j * tile
-                    query_row = lax.broadcasted_iota(jnp.int32, (tile, tile), 1) + i * tile
-                    apart = delta * rows + key_row - query_row
-                    usable = mask[j * tile : (j + 1) * tile] >= 0.0
-                    kept = (apart == 0) | ((jnp.abs(apart) <= HALF) & usable)
-                    scores = jnp.where(kept, scores, masked_score)
-                column.append(scores)
-            column = jnp.concatenate(column, axis=0)
-            old = peak[:, across]
-            new = jnp.maximum(old, jnp.max(column, axis=0, keepdims=True))
-            probs_buf[:, across] = jnp.exp2(column - new).astype(jnp.bfloat16)
-            peak[:, across] = new
-            shrinks.append(jnp.exp2(old - new))
-        shrink = jnp.concatenate(shrinks, axis=1)
-        weighted[...] = weighted[...] * shrink + jnp.dot(
-            values, probs_buf[...], preferred_element_type=jnp.float32
-        )
+        for span in spans:
+            shrinks = []
+            for i in range(span.start // tile, span.stop // tile):
+                across = slice(i * tile, (i + 1) * tile)
+                column = []
+                highs = []
+                for j in range(tiles):
+                    down = slice(j * tile, (j + 1) * tile)
+                    offset = jnp.clip(delta * tiles + (j - i) + offsets // 2, 0, offsets - 1)
+                    scores = scores_buf[down, across] + table[codes_ref[i, offset]]
+                    if special:
+                        key_row = lax.broadcasted_iota(jnp.int32, (tile, tile), 0) + j * tile
+                        query_row = lax.broadcasted_iota(jnp.int32, (tile, tile), 1) + i * tile
+                        apart = delta * rows + key_row - query_row
+                        usable = mask[source, down].astype(jnp.float32) >= 0.0
+                        kept = (apart == 0) | ((jnp.abs(apart) <= HALF) & usable)
+                        scores = jnp.where(kept, scores, masked_score)
+                    column.append(scores)
+                    highs.append(jnp.max(scores.reshape(tile // 8, 8, tile), axis=0))
+                while len(highs) > 1:
+                    highs = [jnp.maximum(u, v) for u, v in zip(highs[::2], highs[1::2])]
+                old = peak[:, across]
+                new = jnp.maximum(old, jnp.max(highs[0], axis=0, keepdims=True))
+                for j in range(tiles):
+                    probs_buf[j * tile : (j + 1) * tile, across] = jnp.exp2(
+                        column[j] - new
+                    ).astype(jnp.bfloat16)
+                peak[:, across] = new
+                shrinks.append(jnp.exp2(old - new))
+            shrink = jnp.concatenate(shrinks, axis=1)
+            weighted[:, span] = weighted[:, span] * shrink + jnp.dot(
+                values, probs_buf[:, span], preferred_element_type=jnp.float32
+            )
 
     def absorb_block(source):
         apart = jnp.abs(source - me)
@@ -540,12 +568,13 @@
             pltpu.VMEM((half_rows, channels), bf16),
             pltpu.VMEM(contact_tiles.shape, f32),
             pltpu.VMEM((2 * HDIM, rows), bf16),
+            pltpu.VMEM((count, rows, HDIM), bf16),
             pltpu.VMEM((rows, rows), f32),
             pltpu.VMEM((rows, rows), bf16),
             pltpu.VMEM((count, rows // tile, 2 * tile, HDIM), bf16),
             pltpu.VMEM((1, rows), f32),
             pltpu.VMEM((HDIM + 16, rows), f32),
-            pltpu.SemaphoreType.DMA((8,)),
+            pltpu.SemaphoreType.DMA((5 + hidden // 256,)),
             pltpu.SemaphoreType.DMA((2,)),
             pltpu.SemaphoreType.DMA((2,)),
             pltpu.SemaphoreType.DMA((4, (2 * far + 1) * columns, 2)),

time: 42.2 us -> 44.8 us (1.062)
  Pallas kernels: 40.1 us -> 42.8 us
    pallas_call x1, Pallas kernels: 40.1 us -> 42.8 us  [per_device(): pl.pallas_call(functools.partial(layer_kernel, columns, count), out_shape...]
where the time goes in v5:
time: 44.8 us; the launch traced here: 44.4 us
  Pallas kernels  42.8 us (96%)
  local copies, waits for them, and re-layouts  1.57 us (4%)
    pallas_call x1, Pallas kernels, per_device(): pl.pallas_call(functools.partial(layer_kernel, columns, count), out_shape...  42.8 us
    unnamed x1, local copies, waits for them, and re-layouts  1.57 us

profile of v5, /device:TPU:18, one launch (start us, length us, event | category | flops | bytes accessed | tf_op | source)
XLA Modules:
  0.0 44.4 jit_solution(7925891686803965429)
XLA Ops:
  0.0 42.8 %shard_map.82 = bf16[512,128]{1,0:T(8,128)(2,1)} custom-call(bf16[512,1536]{1,0:T(8,128)(2,1)} %act_hbm.1, bf16[3,1536,768]{2,1,0:T(8,128)(2,1)} %taps_hbm.1, bf16[768,1536]{1,0:T(8,128)(2,1)} %mix_hbm.1, bf16[1536,128]{1,0:T(8,128)(2,1)} %wq_hbm.1, bf16[1536,256]{1,0:T(8,128)(2,1)} %wkv_hbm.1, bf16[16,128,128]{2,1,0:T(8,128)(2,1)} %tiles_ref.1, ...), custom_call_target="tpu_custom_call" | custom-call | flops 7583301632 | bytes 14680064 | tf_op jit(solution)/shard_map/pallas_call | solution.py:553
  42.8 1.6 %copy.10 = bf16[512,128]{1,0:T(8,128)(2,1)} copy(bf16[512,128]{1,0:T(8,128)(2,1)} %shard_map.82) | data formatting | bytes 262144

commit v6 on v5

--- a/solution.py
+++ b/solution.py
@@ -136,10 +136,13 @@
     mix_hbm,
     wq_hbm,
     wkv_hbm,
+    tiles_hbm,
+    codes_hbm,
+    valid_hbm,
+    out_ref,
     tiles_ref,
     codes_ref,
     valid_ref,
-    out_ref,
     act,
     taps,
     mix,
@@ -152,7 +155,6 @@
     normed,
     table,
     queries,
-    mask,
     scores_buf,
     probs_buf,
     kvbuf,
@@ -187,18 +189,21 @@
             load_sem.at[1],
         ),
     ]
-    tap_loads = []
-    for p in range(parts):
-        cols = pl.ds(p * wide, wide)
-        tap_loads.append(
-            pltpu.make_async_copy(taps_hbm.at[:, :, cols], taps.at[:, :, cols], load_sem.at[5 + p])
-        )
+    tap_loads = [
+        pltpu.make_async_copy(taps_hbm.at[tap], taps.at[tap], load_sem.at[5 + tap])
+        for tap in range(3)
+    ]
     late_loads = [
         pltpu.make_async_copy(mix_hbm, mix, load_sem.at[2]),
         pltpu.make_async_copy(wkv_hbm, wkv, load_sem.at[3]),
         pltpu.make_async_copy(wq_hbm, wq, load_sem.at[4]),
     ]
-    for load in loads:
+    small_loads = [
+        pltpu.make_async_copy(tiles_hbm, tiles_ref, load_sem.at[8]),
+        pltpu.make_async_copy(codes_hbm, codes_ref, load_sem.at[9]),
+        pltpu.make_async_copy(valid_hbm, valid_ref, load_sem.at[10]),
+    ]
+    for load in loads + tap_loads + late_loads + small_loads:
         load.start()
 
     barrier = pltpu.get_barrier_semaphore()
@@ -217,8 +222,6 @@
             pl.semaphore_signal(barrier, inc=1, device_id={"seq": target}, device_id_type=MESH)
 
     loads[0].wait()
-    for load in tap_loads + late_loads:
-        load.start()
     loads[1].wait()
     pl.semaphore_wait(barrier, sum(ok.astype(jnp.int32) for ok, _target in greeted))
 
@@ -263,7 +266,7 @@
         return carry
 
     def turn_tile(code):
-        table[code] = tiles_ref[code].astype(jnp.float32).T * LOG2E
+        table[code] = tiles_ref[code].T.astype(jnp.float32) * LOG2E
 
     lax.fori_loop(0, early_rows // (2 * edge), lift_strip, 0)
 
@@ -279,28 +282,6 @@
         def _():
             lifted[at : at + edge] = jnp.zeros((edge, channels), jnp.bfloat16)
 
-    for code in range(tiles_ref.shape[0]):
-        turn_tile(code)
-
-    def mask_of(d, carry):
-        source = me + d - place.reach
-
-        @pl.when((source >= 0) & (source < count))
-        def _():
-            line = [valid_ref[pl.ds(source * tiles + j, 1)] for j in range(tiles)]
-            line = jnp.where(jnp.concatenate(line, axis=1) == 1, 0.0, masked_score)
-            line = jnp.broadcast_to(line, (16, rows)).astype(jnp.bfloat16)
-            spread = lax.dot_general(
-                line,
-                jnp.ones((16, HDIM), jnp.bfloat16),
-                (((0,), (0,)), ((), ())),
-                preferred_element_type=jnp.float32,
-            )
-            mask[source] = spread.astype(jnp.bfloat16)
-
-        return carry
-
-    lax.fori_loop(0, 2 * place.reach + 1, mask_of, 0)
     lift_halo(0, has_prev, to_next)
     lift_halo(1, has_next, to_prev)
 
@@ -342,8 +323,6 @@
         at = half * half_rows
         for p in range(parts):
             cols = slice(p * wide, (p + 1) * wide)
-            if half == 0:
-                tap_loads[p].wait()
             low = jnp.dot(
                 lifted[at : at + tall], taps[0, :, cols], preferred_element_type=jnp.float32
             )
@@ -392,6 +371,8 @@
         queries[:HDIM, here] = query
 
     beside = [functools.partial(lift, at, edge) for at in range(early_rows, rows, edge)]
+    for load in tap_loads:
+        load.wait()
     convolve(0, beside)
     for load in late_loads:
         load.wait()
@@ -399,16 +380,29 @@
     convolve(1, [])
     lax.fori_loop(0, place.near(), hand_one, 0)
     project(1)
+    for load in small_loads:
+        load.wait()
+    for code in range(tiles_ref.shape[0]):
+        turn_tile(code)
 
     def absorb(source, special):
         delta = source - me
         keys = jnp.concatenate([kvbuf[source, j, :tile] for j in range(tiles)], axis=0)
         values = jnp.concatenate([kvbuf[source, j, tile:] for j in range(tiles)], axis=1)
         values = jnp.concatenate([values, jnp.ones((16, rows), jnp.bfloat16)], axis=0)
+        line = [valid_ref[pl.ds(source * tiles + j, 1)] for j in range(tiles)]
+        line = jnp.where(jnp.concatenate(line, axis=1) == 1, 0.0, masked_score)
+        line = jnp.broadcast_to(line, (16, rows)).astype(jnp.bfloat16)
+        mask = lax.dot_general(
+            line,
+            jnp.ones((16, HDIM), jnp.bfloat16),
+            (((0,), (0,)), ((), ())),
+            preferred_element_type=jnp.float32,
+        )
         if special:
             looked = queries.at[:HDIM]
         else:
-            keys = jnp.concatenate([keys, mask[source]], axis=1)
+            keys = jnp.concatenate([keys, mask.astype(jnp.bfloat16)], axis=1)
             looked = queries
         spans = [slice(n, n + 2 * tile) for n in range(0, rows, 2 * tile)]
         for span in spans:
@@ -429,7 +423,7 @@
                         key_row = lax.broadcasted_iota(jnp.int32, (tile, tile), 0) + j * tile
                         query_row = lax.broadcasted_iota(jnp.int32, (tile, tile), 1) + i * tile
                         apart = delta * rows + key_row - query_row
-                        usable = mask[source, down].astype(jnp.float32) >= 0.0
+                        usable = mask[down] >= 0.0
                         kept = (apart == 0) | ((jnp.abs(apart) <= HALF) & usable)
                         scores = jnp.where(kept, scores, masked_score)
                     column.append(scores)
@@ -547,15 +541,17 @@
     far = -(-(HALF // rows) // plane)
     valid = bin_valid.reshape(count * rows // tile, tile)
     vmem = pl.BlockSpec(memory_space=pltpu.VMEM)
-    smem = pl.BlockSpec(memory_space=pltpu.SMEM)
     hbm = pl.BlockSpec(memory_space=pl.ANY)
     bf16, f32 = jnp.bfloat16, jnp.float32
     return pl.pallas_call(
         functools.partial(layer_kernel, columns, count),
         out_shape=jax.ShapeDtypeStruct((rows, HDIM), bf16),
-        in_specs=[hbm, hbm, hbm, hbm, hbm, vmem, smem, vmem],
+        in_specs=[hbm] * 8,
         out_specs=vmem,
         scratch_shapes=[
+            pltpu.VMEM(contact_tiles.shape, bf16),
+            pltpu.SMEM(tile_codes.shape, jnp.int32),
+            pltpu.VMEM(valid.shape, jnp.int32),
             pltpu.VMEM(activations.shape, bf16),
             pltpu.VMEM(dilated_tap_weight.shape, bf16),
             pltpu.VMEM(conv_mix.shape, bf16),
@@ -568,13 +564,12 @@
             pltpu.VMEM((half_rows, channels), bf16),
             pltpu.VMEM(contact_tiles.shape, f32),
             pltpu.VMEM((2 * HDIM, rows), bf16),
-            pltpu.VMEM((count, rows, HDIM), bf16),
             pltpu.VMEM((rows, rows), f32),
             pltpu.VMEM((rows, rows), bf16),
             pltpu.VMEM((count, rows // tile, 2 * tile, HDIM), bf16),
             pltpu.VMEM((1, rows), f32),
             pltpu.VMEM((HDIM + 16, rows), f32),
-            pltpu.SemaphoreType.DMA((5 + hidden // 256,)),
+            pltpu.SemaphoreType.DMA((11,)),
             pltpu.SemaphoreType.DMA((2,)),
             pltpu.SemaphoreType.DMA((2,)),
             pltpu.SemaphoreType.DMA((4, (2 * far + 1) * columns, 2)),

time: 44.8 us -> 44.2 us (0.987)
  Pallas kernels: 42.8 us -> 42.2 us
    pallas_call x1, Pallas kernels: 42.8 us -> 42.2 us  [per_device(): pl.pallas_call(functools.partial(layer_kernel, columns, count), out_shape...]
where the time goes in v6:
time: 44.2 us; the launch traced here: 43.8 us
  Pallas kernels  42.2 us (95%)
  local copies, waits for them, and re-layouts  1.57 us (4%)
    pallas_call x1, Pallas kernels, per_device(): pl.pallas_call(functools.partial(layer_kernel, columns, count), out_shape...  42.2 us
    unnamed x1, local copies, waits for them, and re-layouts  1.57 us

profile of v6, /device:TPU:18, one launch (start us, length us, event | category | flops | bytes accessed | tf_op | source)
XLA Modules:
  0.0 43.8 jit_solution(13189326833492524163)
XLA Ops:
  0.0 42.2 %shard_map.82 = bf16[512,128]{1,0:T(8,128)(2,1)} custom-call(bf16[512,1536]{1,0:T(8,128)(2,1)} %act_hbm.1, bf16[3,1536,768]{2,1,0:T(8,128)(2,1)} %taps_hbm.1, bf16[768,1536]{1,0:T(8,128)(2,1)} %mix_hbm.1, bf16[1536,128]{1,0:T(8,128)(2,1)} %wq_hbm.1, bf16[1536,256]{1,0:T(8,128)(2,1)} %wkv_hbm.1, bf16[16,128,128]{2,1,0:T(8,128)(2,1)} %tiles_hbm.1, ...), custom_call_target="tpu_custom_call" | custom-call | flops 7583301632 | bytes 14680064 | tf_op jit(solution)/shard_map/pallas_call | solution.py:546
  42.2 1.6 %copy.10 = bf16[512,128]{1,0:T(8,128)(2,1)} copy(bf16[512,128]{1,0:T(8,128)(2,1)} %shard_map.82) | data formatting | bytes 262144

commit v7 on v6

--- a/solution.py
+++ b/solution.py
@@ -55,11 +55,14 @@
         blocks = self.order()
         first = self.near()
         steps = [(0, k, 0) for k in range(1, first + 1)]
-        steps += [(2, k, 1) for k in range(1, first + 1)]
+        steps += [(1, k, 1) for k in range(1, first + 1)]
         for k in range(first + 1, len(blocks), 2):
-            early = 2 if self.columns == 2 and k == first + 1 else 0
-            steps += [(2 * k - 2 - early, k, 0), (2 * k - 2 - early, k + 1, 0)]
-            steps += [(2 * k - early, k, 1), (2 * k - early, k + 1, 1)]
+            turn, later = 2 * k - 4, 2 * k - 2
+            if self.columns == 2 and k == first + 1:
+                turn, later = 2, 6
+            elif self.columns == 2 and k == first + 3:
+                turn, later = 6, 8
+            steps += [(turn, k, 0), (turn, k + 1, 0), (later, k, 1), (later, k + 1, 1)]
         return steps
 
     def near(self):
@@ -283,7 +286,6 @@
             lifted[at : at + edge] = jnp.zeros((edge, channels), jnp.bfloat16)
 
     lift_halo(0, has_prev, to_next)
-    lift_halo(1, has_next, to_prev)
 
     def moves_of(k, half):
         dz, flip = place.step(k)
@@ -371,19 +373,19 @@
         queries[:HDIM, here] = query
 
     beside = [functools.partial(lift, at, edge) for at in range(early_rows, rows, edge)]
-    for load in tap_loads:
+    beside += [functools.partial(turn_tile, code) for code in range(tiles_ref.shape[0])]
+    for load in tap_loads + small_loads[:1]:
         load.wait()
     convolve(0, beside)
     for load in late_loads:
         load.wait()
     project(0)
+    lift_halo(1, has_next, to_prev)
     convolve(1, [])
     lax.fori_loop(0, place.near(), hand_one, 0)
     project(1)
-    for load in small_loads:
+    for load in small_loads[1:]:
         load.wait()
-    for code in range(tiles_ref.shape[0]):
-        turn_tile(code)
 
     def absorb(source, special):
         delta = source - me
@@ -419,13 +421,16 @@
                     down = slice(j * tile, (j + 1) * tile)
                     offset = jnp.clip(delta * tiles + (j - i) + offsets // 2, 0, offsets - 1)
                     scores = scores_buf[down, across] + table[codes_ref[i, offset]]
-                    if special:
-                        key_row = lax.broadcasted_iota(jnp.int32, (tile, tile), 0) + j * tile
-                        query_row = lax.broadcasted_iota(jnp.int32, (tile, tile), 1) + i * tile
+                    if special and i == j:
+                        key_row = lax.broadcasted_iota(jnp.int32, (tile, tile), 0)
+                        query_row = lax.broadcasted_iota(jnp.int32, (tile, tile), 1)
                         apart = delta * rows + key_row - query_row
-                        usable = mask[down] >= 0.0
-                        kept = (apart == 0) | ((jnp.abs(apart) <= HALF) & usable)
+                        kept = (apart == 0) | ((jnp.abs(apart) <= HALF) & (mask[down] >= 0.0))
                         scores = jnp.where(kept, scores, masked_score)
+                    elif special:
+                        away = jnp.abs(delta * tiles + (j - i))
+                        scores = scores + mask[down]
+                        scores = scores + jnp.where(away <= HALF // tile, 0.0, masked_score)
                     column.append(scores)
                     highs.append(jnp.max(scores.reshape(tile // 8, 8, tile), axis=0))
                 while len(highs) > 1:

time: 44.2 us -> 41.3 us (0.934)
  Pallas kernels: 42.2 us -> 39.6 us
    pallas_call x1, Pallas kernels: 42.2 us -> 39.6 us  [per_device(): pl.pallas_call(functools.partial(layer_kernel, columns, count), out_shape...]
where the time goes in v7:
time: 41.3 us; the launch traced here: 41.1 us
  Pallas kernels  39.6 us (96%)
  local copies, waits for them, and re-layouts  1.57 us (4%)
    pallas_call x1, Pallas kernels, per_device(): pl.pallas_call(functools.partial(layer_kernel, columns, count), out_shape...  39.6 us
    unnamed x1, local copies, waits for them, and re-layouts  1.57 us

profile of v7, /device:TPU:18, one launch (start us, length us, event | category | flops | bytes accessed | tf_op | source)
XLA Modules:
  0.0 41.1 jit_solution(12327542373671563826)
XLA Ops:
  0.0 39.6 %shard_map.82 = bf16[512,128]{1,0:T(8,128)(2,1)} custom-call(bf16[512,1536]{1,0:T(8,128)(2,1)} %act_hbm.1, bf16[3,1536,768]{2,1,0:T(8,128)(2,1)} %taps_hbm.1, bf16[768,1536]{1,0:T(8,128)(2,1)} %mix_hbm.1, bf16[1536,128]{1,0:T(8,128)(2,1)} %wq_hbm.1, bf16[1536,256]{1,0:T(8,128)(2,1)} %wkv_hbm.1, bf16[16,128,128]{2,1,0:T(8,128)(2,1)} %tiles_hbm.1, ...), custom_call_target="tpu_custom_call" | custom-call | flops 7583301632 | bytes 14680064 | tf_op jit(solution)/shard_map/pallas_call | solution.py:551
  39.6 1.6 %copy.10 = bf16[512,128]{1,0:T(8,128)(2,1)} copy(bf16[512,128]{1,0:T(8,128)(2,1)} %shard_map.82) | data formatting | bytes 262144

commit v8 on v7

--- a/solution.py
+++ b/solution.py
@@ -581,7 +581,7 @@
             pltpu.SemaphoreType.DMA((count, 2)),
         ],
         compiler_params=pltpu.CompilerParams(
-            collective_id=0, has_side_effects=True, vmem_limit_bytes=56 * 1024 * 1024
+            collective_id=0, has_side_effects=True, vmem_limit_bytes=55040 * 1024
         ),
         cost_estimate=pl.CostEstimate(
             flops=2 * rows * channels * (4 * hidden + 3 * HDIM) + 4 * rows * HDIM * 2 * HALF,

time: 41.3 us -> 41.2 us (level)
  Pallas kernels: 39.6 us -> 38.9 us
  local copies, waits for them, and re-layouts: 1.57 us -> 2.1 us
    pallas_call x1, Pallas kernels: 39.6 us -> 38.9 us  [per_device(): pl.pallas_call(functools.partial(layer_kernel, columns, count), out_shape...]
    unnamed x1 -> x5, local copies, waits for them, and re-layouts: 1.57 us -> 2.1 us
where the time goes in v8:
time: 41.2 us; the launch traced here: 41 us
  Pallas kernels  38.9 us (94%)
  local copies, waits for them, and re-layouts  2.1 us (5%)
    pallas_call x1, Pallas kernels, per_device(): pl.pallas_call(functools.partial(layer_kernel, columns, count), out_shape...  38.9 us
    unnamed x5, local copies, waits for them, and re-layouts  2.1 us

profile of v8, /device:TPU:18, one launch (start us, length us, event | category | flops | bytes accessed | tf_op | source)
XLA Modules:
  0.0 41.0 jit_solution(185461283517921610)
XLA Ops:
  0.0 0.0 copy-start
  0.0 0.8 %copy-done = s32[8192]{0:T(1024)S(1)} copy-done((s32[8192]{0:T(1024)S(1)}, s32[8192]{0:T(1024)}, u32[]{:S(2)}) %copy-start) | copy-done | bytes 32792
  0.8 0.0 copy-start.1
  0.8 0.7 %copy-done.1 = s32[4,65]{1,0:T(4,128)S(1)} copy-done((s32[4,65]{1,0:T(4,128)S(1)}, s32[4,65]{1,0:T(4,128)}, u32[]{:S(2)}) %copy-start.1) | copy-done | bytes 1064
  1.4 38.9 %shard_map.82 = bf16[512,128]{1,0:T(8,128)(2,1)S(1)} custom-call(bf16[512,1536]{1,0:T(8,128)(2,1)} %act_hbm.1, bf16[3,1536,768]{2,1,0:T(8,128)(2,1)} %taps_hbm.1, bf16[768,1536]{1,0:T(8,128)(2,1)} %mix_hbm.1, bf16[1536,128]{1,0:T(8,128)(2,1)} %wq_hbm.1, bf16[1536,256]{1,0:T(8,128)(2,1)} %wkv_hbm.1, bf16[16,128,128]{2,1,0:T(8,128)(2,1)} %tiles_hbm.1, ...), custom_call_target="tpu_custom_call" | custom-call | flops 7583301632 | bytes 14680064 | tf_op jit(solution)/shard_map/pallas_call | solution.py:551
  40.4 0.7 %copy.10 = bf16[512,128]{1,0:T(8,128)(2,1)} copy(bf16[512,128]{1,0:T(8,128)(2,1)S(1)} %shard_map.82) | data formatting | bytes 262144
Async XLA Ops:
  0.0 0.8 %copy-start = (s32[8192]{0:T(1024)S(1)}, s32[8192]{0:T(1024)}, u32[]{:S(2)}) copy-start(s32[8192]{0:T(1024)} %param.15) | copy-start | bytes 98308
  0.8 0.7 %copy-start.1 = (s32[4,65]{1,0:T(4,128)S(1)}, s32[4,65]{1,0:T(4,128)}, u32[]{:S(2)}) copy-start(s32[4,65]{1,0:T(4,128)} %codes_hbm.1) | copy-start | bytes 3124
